TPU v7x, 128 devices: a whole 4x4x4 slice. The times are simulated.
128 devices in a mesh: blk: 64 (over y, z, x_hi, core), rep: 2 (over x_lo).
Axes of the slice: x: 4 (x_hi: 2, x_lo: 2; x = x_hi * 2 + x_lo), y: 4, z: 4, core: 2. Of those that a mesh axis runs over, the one named last changes fastest.
Arguments:
- picture_vectors: float32 [2, 32768, 1152], P('rep', 'blk'), may hold values from -0.2 to 0.2
- caption_vectors: float32 [2, 32768, 1152], P('rep', 'blk'), may hold values from -0.2 to 0.2
- scale_exponent: float32 [], replicated, may hold values from 2 to 2.5
- offset_shift: float32 [], replicated, may hold values from -6 to -4
Outputs:
- picture_deriv: float32 [2, 32768, 1152], P('rep', 'blk')
- caption_deriv: float32 [2, 32768, 1152], P('rep', 'blk')
- objective_value: float32 [], replicated
- scale_exponent_deriv: float32 [], replicated
- offset_shift_deriv: float32 [], replicated
All inputs are finite; a program needn't handle non-finite values.
Results may differ from a plain program's by a relative error of at most 0.00019.
Values sent between devices are 32-bit elements; how exact they have to be, the bound alone decides.
A program may use at most 192 MiB of HBM per device.

v0:
```python
import jax
import jax.numpy as jnp
from jax import lax
from jax.sharding import PartitionSpec as P

STEPS = 8


EPSILON = 1e-06


def from_behind(block, axis, distance):
    devices = range(lax.axis_size(axis))
    route = [((i - distance) % len(devices), i) for i in devices]
    return lax.ppermute(block, axis, route)


def unit_rows(vector):
    row_norm = jnp.sqrt(jnp.sum(vector * vector, axis=-1, keepdims=True) + EPSILON)
    return (vector / row_norm, row_norm)


def unit_backward(grad_unit, unit, row_norm):
    return (grad_unit - unit * jnp.sum(unit * grad_unit, axis=-1, keepdims=True)) / row_norm


def shards(picture_vectors, caption_vectors, scale_exponent, offset_shift):
    picture_unitlength, image_norm = unit_rows(picture_vectors[0])
    text_unit, text_norm = unit_rows(caption_vectors[0])
    row_count = picture_unitlength.shape[0]
    odds_multiplier = jnp.exp(scale_exponent)
    diagonal_mask = lax.broadcasted_iota(
        jnp.int32, (row_count, row_count), 0
    ) == lax.broadcasted_iota(jnp.int32, (row_count, row_count), 1)
    label_home = jnp.where(diagonal_mask, 1.0, -1.0).astype(jnp.float32)
    arriving_caption_matrix = text_unit
    picture_running_buffer = jnp.zeros_like(picture_unitlength)
    text_acc = jnp.zeros_like(text_unit)
    loss_part = jnp.float32(0.0)
    cos_part = jnp.float32(0.0)
    bias_part = jnp.float32(0.0)
    for cycle_step in range(STEPS):
        if cycle_step > 0:
            arriving_caption_matrix = from_behind(arriving_caption_matrix, "blk", 1)
        angular_closeness = lax.dot_general(
            picture_unitlength,
            arriving_caption_matrix,
            (((1,), (1,)), ((), ())),
            precision=lax.Precision.HIGHEST,
            preferred_element_type=jnp.float32,
        )
        match_sign_target = label_home if cycle_step == 0 else -1.0
        oriented_odds = match_sign_target * (odds_multiplier * angular_closeness + offset_shift)
        loss_part = loss_part + jnp.sum(jax.nn.softplus(-oriented_odds))
        steepness_weight = -match_sign_target * jax.nn.sigmoid(-oriented_odds)
        cos_part = cos_part + jnp.sum(steepness_weight * angular_closeness)
        bias_part = bias_part + jnp.sum(steepness_weight)
        picture_running_buffer = picture_running_buffer + odds_multiplier * jnp.dot(
            steepness_weight,
            arriving_caption_matrix,
            precision=lax.Precision.HIGHEST,
            preferred_element_type=jnp.float32,
        )
        caption_share = odds_multiplier * lax.dot_general(
            steepness_weight,
            picture_unitlength,
            (((0,), (0,)), ((), ())),
            precision=lax.Precision.HIGHEST,
            preferred_element_type=jnp.float32,
        )
        if cycle_step == 0:
            text_acc = caption_share
        else:
            text_acc = from_behind(text_acc, "blk", 1) + caption_share
    text_acc = from_behind(text_acc, "blk", -(STEPS - 1))
    loss_sum, angular_running_aggregate, bias_sum = lax.psum(
        (loss_part, cos_part, bias_part), ("blk", "rep")
    )
    matched_number = row_count * lax.axis_size("blk") * lax.axis_size("rep")
    picture_deriv = unit_backward(picture_running_buffer, picture_unitlength, image_norm)
    caption_deriv = unit_backward(text_acc, text_unit, text_norm)
    objective_value = loss_sum / matched_number
    scale_exponent_deriv = odds_multiplier * angular_running_aggregate / matched_number
    offset_shift_deriv = bias_sum / matched_number
    return (
        picture_deriv[None],
        caption_deriv[None],
        objective_value,
        scale_exponent_deriv,
        offset_shift_deriv,
    )


def solution(mesh):
    placed = (P("rep", "blk", None), P("rep", "blk", None), P(), P())
    return jax.shard_map(
        shards,
        mesh=mesh,
        in_specs=placed,
        out_specs=(P("rep", "blk", None), P("rep", "blk", None), P(), P(), P()),
        check_vma=False,
    )
```

profile of v0, /device:TPU:0, one launch (start us, length us, event | category | flops | bytes accessed | tf_op | source)
XLA Modules:
  0.0 504.1 jit_solution(16249853237793487360)
XLA Ops:
  0.6 2.0 fusion.4
  3.0 1.6 bitcast_divide_fusion
  6.0 2.0 fusion.6
  8.4 6.0 %fusion.27 = (f32[]{:T(128)}, f32[]{:T(128)}, f32[]{:T(128)}, f32[512,512]{1,0:T(8,128)S(1)}) fusion(f32[]{:T(128)S(6)} %copy.10, f32[]{:T(128)S(6)} %exp.52, f32[1,512,1152]{2,1,0:T(8,128)S(1)} %copy-done, f32[512]{0:T(512)S(1)} %add_sqrt_fusion, f32[1,512,1152]{2,1,0:T(8,128)S(1)} %copy-done.1, f32[512]{0:T(512)S(1)} %add_sqrt_fusion.1), kind=kOutput, calls=%fused_computation.85 | convolution fusion | flops 3630301184 | bytes 5771284 | tf_op jit(solution)/shard_map/dot_general | solution.py:45
  14.4 4.9 convolution_multiply_fusion.7
  19.3 3.3 collective-permute-start.7
  22.6 17.4 %collective-permute-done = f32[512,1152]{1,0:T(8,128)} collective-permute-done((f32[512,1152]{1,0:T(8,128)}, f32[512,1152]{1,0:T(8,128)}, u32[]{:S(2)}, u32[]{:S(2)}) %collective-permute-start) | collective-permute-done | bytes 2359328 | tf_op jit(solution)/shard_map/ppermute | solution.py:15
  40.2 7.6 %fusion.21 = (f32[]{:T(128)}, f32[]{:T(128)}, f32[]{:T(128)}, f32[512,512]{1,0:T(8,128)S(1)}) fusion(f32[]{:T(128)S(6)} %copy.10, f32[]{:T(128)S(6)} %exp.52, f32[512,1152]{1,0:T(8,128)} %collective-permute-done, f32[1,512,1152]{2,1,0:T(8,128)S(1)} %copy-done.1, f32[512]{0:T(512)S(1)} %add_sqrt_fusion.1), kind=kOutput, calls=%fused_computation.79 | convolution fusion | flops 3628662784 | bytes 5769236 | tf_op jit(solution)/shard_map/dot_general | solution.py:45
  47.8 17.4 %collective-permute-done.7 = f32[512,1152]{1,0:T(8,128)S(1)} collective-permute-done((f32[512,1152]{1,0:T(8,128)S(1)}, f32[512,1152]{1,0:T(8,128)S(1)}, u32[]{:S(2)}, u32[]{:S(2)}) %collective-permute-start.7) | collective-permute-done | bytes 2359328 | tf_op jit(solution)/shard_map/ppermute | solution.py:15
  65.1 5.0 fusion
  70.2 20.2 %collective-permute-done.1 = f32[512,1152]{1,0:T(8,128)S(1)} collective-permute-done((f32[512,1152]{1,0:T(8,128)}, f32[512,1152]{1,0:T(8,128)S(1)}, u32[]{:S(2)}, u32[]{:S(2)}) %collective-permute-start.1) | collective-permute-done | bytes 2359328 | tf_op jit(solution)/shard_map/ppermute | solution.py:15
  90.8 5.9 %fusion.22 = (f32[]{:T(128)}, f32[]{:T(128)}, f32[]{:T(128)}, f32[512,512]{1,0:T(8,128)S(1)}) fusion(f32[]{:T(128)S(6)} %copy.10, f32[]{:T(128)S(6)} %exp.52, f32[512,1152]{1,0:T(8,128)S(1)} %collective-permute-done.1, f32[1,512,1152]{2,1,0:T(8,128)S(1)} %copy-done.1, f32[512]{0:T(512)S(1)} %add_sqrt_fusion.1), kind=kOutput, calls=%fused_computation.80 | convolution fusion | flops 3628662784 | bytes 5769236 | tf_op jit(solution)/shard_map/dot_general | solution.py:45
  96.7 4.9 convolution_multiply_fusion.5
  101.6 14.1 %collective-permute-done.8 = f32[512,1152]{1,0:T(8,128)S(1)} collective-permute-done((f32[512,1152]{1,0:T(8,128)S(1)}, f32[512,1152]{1,0:T(8,128)S(1)}, u32[]{:S(2)}, u32[]{:S(2)}) %collective-permute-start.8) | collective-permute-done | bytes 2359328 | tf_op jit(solution)/shard_map/ppermute | solution.py:15
  116.0 25.0 %collective-permute-done.2 = f32[512,1152]{1,0:T(8,128)S(1)} collective-permute-done((f32[512,1152]{1,0:T(8,128)S(1)}, f32[512,1152]{1,0:T(8,128)S(1)}, u32[]{:S(2)}, u32[]{:S(2)}) %collective-permute-start.2) | collective-permute-done | bytes 2359328 | tf_op jit(solution)/shard_map/ppermute | solution.py:15
  141.1 5.9 %fusion.23 = (f32[]{:T(128)}, f32[]{:T(128)}, f32[]{:T(128)}, f32[512,512]{1,0:T(8,128)S(1)}) fusion(f32[]{:T(128)S(6)} %copy.10, f32[]{:T(128)S(6)} %exp.52, f32[512,1152]{1,0:T(8,128)S(1)} %collective-permute-done.2, f32[1,512,1152]{2,1,0:T(8,128)S(1)} %copy-done.1, f32[512]{0:T(512)S(1)} %add_sqrt_fusion.1), kind=kOutput, calls=%fused_computation.81 | convolution fusion | flops 3628662784 | bytes 5769236 | tf_op jit(solution)/shard_map/dot_general | solution.py:45
  147.1 4.9 convolution_multiply_fusion.4
  152.0 14.3 %collective-permute-done.9 = f32[512,1152]{1,0:T(8,128)S(1)} collective-permute-done((f32[512,1152]{1,0:T(8,128)S(1)}, f32[512,1152]{1,0:T(8,128)S(1)}, u32[]{:S(2)}, u32[]{:S(2)}) %collective-permute-start.9) | collective-permute-done | bytes 2359328 | tf_op jit(solution)/shard_map/ppermute | solution.py:15
  166.6 25.0 %collective-permute-done.3 = f32[512,1152]{1,0:T(8,128)S(1)} collective-permute-done((f32[512,1152]{1,0:T(8,128)S(1)}, f32[512,1152]{1,0:T(8,128)S(1)}, u32[]{:S(2)}, u32[]{:S(2)}) %collective-permute-start.3) | collective-permute-done | bytes 2359328 | tf_op jit(solution)/shard_map/ppermute | solution.py:15
  191.7 5.9 %fusion.24 = (f32[]{:T(128)}, f32[]{:T(128)}, f32[]{:T(128)}, f32[512,512]{1,0:T(8,128)S(1)}) fusion(f32[]{:T(128)S(6)} %copy.10, f32[]{:T(128)S(6)} %exp.52, f32[512,1152]{1,0:T(8,128)S(1)} %collective-permute-done.3, f32[1,512,1152]{2,1,0:T(8,128)S(1)} %copy-done.1, f32[512]{0:T(512)S(1)} %add_sqrt_fusion.1), kind=kOutput, calls=%fused_computation.82 | convolution fusion | flops 3628662784 | bytes 5769236 | tf_op jit(solution)/shard_map/dot_general | solution.py:45
  197.7 4.9 convolution_multiply_fusion.3
  202.6 14.2 %collective-permute-done.10 = f32[512,1152]{1,0:T(8,128)S(1)} collective-permute-done((f32[512,1152]{1,0:T(8,128)S(1)}, f32[512,1152]{1,0:T(8,128)S(1)}, u32[]{:S(2)}, u32[]{:S(2)}) %collective-permute-start.10) | collective-permute-done | bytes 2359328 | tf_op jit(solution)/shard_map/ppermute | solution.py:15
  217.1 25.1 %collective-permute-done.4 = f32[512,1152]{1,0:T(8,128)} collective-permute-done((f32[512,1152]{1,0:T(8,128)S(1)}, f32[512,1152]{1,0:T(8,128)}, u32[]{:S(2)}, u32[]{:S(2)}) %collective-permute-start.4) | collective-permute-done | bytes 2359328 | tf_op jit(solution)/shard_map/ppermute | solution.py:15
  242.6 7.6 %fusion.25 = (f32[]{:T(128)}, f32[]{:T(128)}, f32[]{:T(128)}, f32[512,512]{1,0:T(8,128)S(1)}) fusion(f32[]{:T(128)S(6)} %copy.10, f32[]{:T(128)S(6)} %exp.52, f32[512,1152]{1,0:T(8,128)} %collective-permute-done.4, f32[1,512,1152]{2,1,0:T(8,128)S(1)} %copy-done.1, f32[512]{0:T(512)S(1)} %add_sqrt_fusion.1), kind=kOutput, calls=%fused_computation.83 | convolution fusion | flops 3628662784 | bytes 5769236 | tf_op jit(solution)/shard_map/dot_general | solution.py:45
  250.2 4.9 convolution_multiply_fusion.2
  255.1 12.3 %collective-permute-done.11 = f32[512,1152]{1,0:T(8,128)S(1)} collective-permute-done((f32[512,1152]{1,0:T(8,128)S(1)}, f32[512,1152]{1,0:T(8,128)S(1)}, u32[]{:S(2)}, u32[]{:S(2)}) %collective-permute-start.11) | collective-permute-done | bytes 2359328 | tf_op jit(solution)/shard_map/ppermute | solution.py:15
  267.4 1.6 add.240
  269.2 7.6 %fusion.29 = f32[512,1152]{1,0:T(8,128)} fusion(f32[512,1152]{1,0:T(8,128)} %bitcast_divide_fusion, f32[512,512]{1,0:T(8,128)S(1)} %get-tuple-element.34, f32[]{:T(128)S(6)} %copy.10, f32[]{:T(128)S(6)} %exp.52), kind=kOutput, calls=%fused_computation.86 | convolution fusion | flops 3626237952 | bytes 5767176 | tf_op jit(solution)/shard_map/dot_general | solution.py:58
  280.5 8.6 %convolution_add_fusion.6 = f32[512,1152]{1,0:T(8,128)} fusion(f32[512,1152]{1,0:T(8,128)} %fusion.29, f32[512,1152]{1,0:T(8,128)} %collective-permute-done, f32[512,512]{1,0:T(8,128)} %copy-done.11, f32[]{:T(128)S(6)} %copy.10, f32[]{:T(128)S(6)} %exp.52), kind=kOutput, calls=%fused_computation.16 | convolution fusion | flops 3625779200 | bytes 8126472 | tf_op jit(solution)/shard_map/dot_general | solution.py:58
  291.0 1.7 collective-permute-done.5
  293.0 8.2 %fusion.26 = (f32[]{:T(128)}, f32[]{:T(128)}, f32[]{:T(128)}, f32[512,512]{1,0:T(8,128)S(1)}) fusion(f32[]{:T(128)S(6)} %copy.10, f32[]{:T(128)S(6)} %exp.52, f32[512,1152]{1,0:T(8,128)} %collective-permute-done.5, f32[1,512,1152]{2,1,0:T(8,128)} %param.4, f32[512]{0:T(512)S(1)} %add_sqrt_fusion.1), kind=kOutput, calls=%fused_computation.84 | convolution fusion | flops 3628662784 | bytes 5769236 | tf_op jit(solution)/shard_map/dot_general | solution.py:45
  302.2 4.9 convolution_multiply_fusion.1
  307.1 10.9 %collective-permute-done.12 = f32[512,1152]{1,0:T(8,128)} collective-permute-done((f32[512,1152]{1,0:T(8,128)}, f32[512,1152]{1,0:T(8,128)}, u32[]{:S(2)}, u32[]{:S(2)}) %collective-permute-start.12) | collective-permute-done | bytes 2359328 | tf_op jit(solution)/shard_map/ppermute | solution.py:15
  318.0 3.4 add.241
  321.9 6.1 %convolution_add_fusion.5 = f32[512,1152]{1,0:T(8,128)} fusion(f32[512,1152]{1,0:T(8,128)S(1)} %copy-done.5, f32[512,1152]{1,0:T(8,128)S(1)} %copy-done.7, f32[512,512]{1,0:T(8,128)S(1)} %get-tuple-element.36, f32[]{:T(128)S(6)} %copy.10, f32[]{:T(128)S(6)} %exp.52), kind=kOutput, calls=%fused_computation.15 | convolution fusion | flops 3625779200 | bytes 8126472 | tf_op jit(solution)/shard_map/dot_general | solution.py:58
  329.9 8.7 %convolution_add_fusion.4 = f32[512,1152]{1,0:T(8,128)} fusion(f32[512,1152]{1,0:T(8,128)} %convolution_add_fusion.5, f32[512,1152]{1,0:T(8,128)} %copy-done.8, f32[512,512]{1,0:T(8,128)} %copy-done.10, f32[]{:T(128)S(6)} %copy.10, f32[]{:T(128)S(6)} %exp.52), kind=kOutput, calls=%fused_computation.14 | convolution fusion | flops 3625779200 | bytes 8126472 | tf_op jit(solution)/shard_map/dot_general | solution.py:58
  340.5 7.4 %convolution_add_fusion.3 = f32[512,1152]{1,0:T(8,128)S(1)} fusion(f32[512,1152]{1,0:T(8,128)} %convolution_add_fusion.4, f32[512,1152]{1,0:T(8,128)} %copy-done.9, f32[512,512]{1,0:T(8,128)S(1)} %copy-done.15, f32[]{:T(128)S(6)} %copy.10, f32[]{:T(128)S(6)} %exp.52), kind=kOutput, calls=%fused_computation.13 | convolution fusion | flops 3625779200 | bytes 8126472 | tf_op jit(solution)/shard_map/dot_general | solution.py:58
  347.9 7.5 %fusion.20 = (f32[]{:T(128)}, f32[]{:T(128)}, f32[]{:T(128)}, f32[512,512]{1,0:T(8,128)S(1)}) fusion(f32[]{:T(128)S(6)} %copy.10, f32[]{:T(128)S(6)} %exp.52, f32[512,1152]{1,0:T(8,128)} %collective-permute-done.6, f32[1,512,1152]{2,1,0:T(8,128)S(1)} %copy-done.3, f32[512]{0:T(512)S(1)} %add_sqrt_fusion.1), kind=kOutput, calls=%fused_computation.78 | convolution fusion | flops 3628662784 | bytes 5769236 | tf_op jit(solution)/shard_map/dot_general | solution.py:45
  355.5 4.9 convolution_multiply_fusion
  360.4 8.2 %collective-permute-done.13 = f32[512,1152]{1,0:T(8,128)} collective-permute-done((f32[512,1152]{1,0:T(8,128)}, f32[512,1152]{1,0:T(8,128)}, u32[]{:S(2)}, u32[]{:S(2)}) %collective-permute-start.13) | collective-permute-done | bytes 2359328 | tf_op jit(solution)/shard_map/ppermute | solution.py:15
  368.6 3.4 add.242
  372.2 7.8 %convolution_add_fusion.2 = f32[512,1152]{1,0:T(8,128)} fusion(f32[512,1152]{1,0:T(8,128)S(1)} %convolution_add_fusion.3, f32[512,1152]{1,0:T(8,128)} %collective-permute-done.4, f32[512,512]{1,0:T(8,128)S(1)} %copy-done.13, f32[]{:T(128)S(6)} %copy.10, f32[]{:T(128)S(6)} %exp.52), kind=kOutput, calls=%fused_computation.12 | convolution fusion | flops 3625779200 | bytes 8126472 | tf_op jit(solution)/shard_map/dot_general | solution.py:58
  385.6 7.9 %convolution_add_fusion.1 = f32[512,1152]{1,0:T(8,128)} fusion(f32[512,1152]{1,0:T(8,128)} %convolution_add_fusion.2, f32[512,1152]{1,0:T(8,128)} %collective-permute-done.5, f32[512,512]{1,0:T(8,128)S(1)} %copy-done.17, f32[]{:T(128)S(6)} %copy.10, f32[]{:T(128)S(6)} %exp.52), kind=kOutput, calls=%fused_computation.11 | convolution fusion | flops 3625779200 | bytes 8126472 | tf_op jit(solution)/shard_map/dot_general | solution.py:58
  393.5 89.0 %all-reduce = (f32[]{:T(128)}, f32[]{:T(128)}, f32[]{:T(128)}) all-reduce(f32[]{:T(128)S(6)} %add.257, f32[]{:T(128)S(6)} %add.264, f32[]{:T(128)S(6)} %add.271), channel_id=1, replica_groups=mesh['blk'=64,'rep'=2] {'blk','rep'}, use_global_device_ids=true, to_apply=%region_12.13 | all-reduce | flops 3 | bytes 24 | tf_op jit(solution)/shard_map/psum | solution.py:76
  484.4 8.5 %multiply_reduce_fusion.1 = (f32[512]{0:T(512)S(1)}, f32[512,1152]{1,0:T(8,128)S(1)}) fusion(f32[512]{0:T(512)S(1)} %add_sqrt_fusion.1, f32[1,512,1152]{2,1,0:T(8,128)} %param.4, f32[]{:T(128)S(6)} %exp.52, f32[512,1152]{1,0:T(8,128)} %convolution_add_fusion.1, f32[512,1152]{1,0:T(8,128)} %collective-permute-done.6, f32[512,512]{1,0:T(8,128)} %copy-done.18, ...), kind=kOutput, calls=%fused_computation.37 | convolution fusion | flops 3628137984 | bytes 10489864 | tf_op jit(solution)/shard_map/dot_general | solution.py:58
  492.9 1.8 divide_bitcast_fusion.1
  494.7 2.0 multiply_reduce_fusion
  496.7 3.5 divide_bitcast_fusion
  (59 shorter events, 5.0 us)
Async XLA Ops:
  0.6 2.4 copy-start
  4.7 35.3 %collective-permute-start = (f32[512,1152]{1,0:T(8,128)}, f32[512,1152]{1,0:T(8,128)}, u32[]{:S(2)}, u32[]{:S(2)}) collective-permute-start(f32[512,1152]{1,0:T(8,128)} %bitcast_divide_fusion), channel_id=1, source_target_pairs={{126,0},{0,2},{2,4},{4,6},{6,8},{8,10},{10,12},{12,14},{14,16},{16... | collective-permute-start | bytes 7077896 | tf_op jit(solution)/shard_map/ppermute | solution.py:15
  6.0 2.4 copy-start.1
  19.3 45.9 %collective-permute-start.7 = (f32[512,1152]{1,0:T(8,128)S(1)}, f32[512,1152]{1,0:T(8,128)S(1)}, u32[]{:S(2)}, u32[]{:S(2)}) collective-permute-start(f32[512,1152]{1,0:T(8,128)S(1)} %convolution_multiply_fusion.7), channel_id=1, source_target_pairs={{126,0},{0,2},{2,4},{4,6},{6,8},{8,10},{10,12},{12,14},{14,16},{16... | collective-permute-start | bytes 7077896 | tf_op jit(solution)/shard_map/ppermute | solution.py:15
  40.0 50.5 %collective-permute-start.1 = (f32[512,1152]{1,0:T(8,128)}, f32[512,1152]{1,0:T(8,128)S(1)}, u32[]{:S(2)}, u32[]{:S(2)}) collective-permute-start(f32[512,1152]{1,0:T(8,128)} %collective-permute-done), channel_id=1, source_target_pairs={{126,0},{0,2},{2,4},{4,6},{6,8},{8,10},{10,12},{12,14},{14,16},{16... | collective-permute-start | bytes 7077896 | tf_op jit(solution)/shard_map/ppermute | solution.py:15
  47.8 22.4 %copy-start.11 = (f32[512,512]{1,0:T(8,128)}, f32[512,512]{1,0:T(8,128)S(1)}, u32[]{:S(2)}) copy-start(f32[512,512]{1,0:T(8,128)S(1)} %get-tuple-element.35) | copy-start | bytes 3145732
  70.1 45.6 %collective-permute-start.8 = (f32[512,1152]{1,0:T(8,128)S(1)}, f32[512,1152]{1,0:T(8,128)S(1)}, u32[]{:S(2)}, u32[]{:S(2)}) collective-permute-start(f32[512,1152]{1,0:T(8,128)S(1)} %fusion), channel_id=1, source_target_pairs={{126,0},{0,2},{2,4},{4,6},{6,8},{8,10},{10,12},{12,14},{14,16},{16... | collective-permute-start | bytes 7077896 | tf_op jit(solution)/shard_map/ppermute | solution.py:15
  90.4 6.3 %copy-start.6 = (f32[512,1152]{1,0:T(8,128)}, f32[512,1152]{1,0:T(8,128)S(1)}, u32[]{:S(2)}) copy-start(f32[512,1152]{1,0:T(8,128)S(1)} %collective-permute-done.1) | copy-start | bytes 7077892
  90.4 50.6 %collective-permute-start.2 = (f32[512,1152]{1,0:T(8,128)S(1)}, f32[512,1152]{1,0:T(8,128)S(1)}, u32[]{:S(2)}, u32[]{:S(2)}) collective-permute-start(f32[512,1152]{1,0:T(8,128)S(1)} %collective-permute-done.1), channel_id=1, source_target_pairs={{126,0},{0,2},{2,4},{4,6},{6,8},{8,10},{10,12},{12,14},{14,16},{16... | collective-permute-start | bytes 7077896 | tf_op jit(solution)/shard_map/ppermute | solution.py:15
  115.9 50.3 %collective-permute-start.9 = (f32[512,1152]{1,0:T(8,128)S(1)}, f32[512,1152]{1,0:T(8,128)S(1)}, u32[]{:S(2)}, u32[]{:S(2)}) collective-permute-start(f32[512,1152]{1,0:T(8,128)S(1)} %add.237), channel_id=1, source_target_pairs={{126,0},{0,2},{2,4},{4,6},{6,8},{8,10},{10,12},{12,14},{14,16},{16... | collective-permute-start | bytes 7077896 | tf_op jit(solution)/shard_map/ppermute | solution.py:15
  141.0 6.1 %copy-start.8 = (f32[512,1152]{1,0:T(8,128)}, f32[512,1152]{1,0:T(8,128)S(1)}, u32[]{:S(2)}) copy-start(f32[512,1152]{1,0:T(8,128)S(1)} %collective-permute-done.2) | copy-start | bytes 7077892
  141.0 50.6 %collective-permute-start.3 = (f32[512,1152]{1,0:T(8,128)S(1)}, f32[512,1152]{1,0:T(8,128)S(1)}, u32[]{:S(2)}, u32[]{:S(2)}) collective-permute-start(f32[512,1152]{1,0:T(8,128)S(1)} %collective-permute-done.2), channel_id=1, source_target_pairs={{126,0},{0,2},{2,4},{4,6},{6,8},{8,10},{10,12},{12,14},{14,16},{16... | collective-permute-start | bytes 7077896 | tf_op jit(solution)/shard_map/ppermute | solution.py:15
  147.1 4.9 copy-start.10
  166.5 50.3 %collective-permute-start.10 = (f32[512,1152]{1,0:T(8,128)S(1)}, f32[512,1152]{1,0:T(8,128)S(1)}, u32[]{:S(2)}, u32[]{:S(2)}) collective-permute-start(f32[512,1152]{1,0:T(8,128)S(1)} %add.238), channel_id=1, source_target_pairs={{126,0},{0,2},{2,4},{4,6},{6,8},{8,10},{10,12},{12,14},{14,16},{16... | collective-permute-start | bytes 7077896 | tf_op jit(solution)/shard_map/ppermute | solution.py:15
  191.5 6.1 %copy-start.9 = (f32[512,1152]{1,0:T(8,128)}, f32[512,1152]{1,0:T(8,128)S(1)}, u32[]{:S(2)}) copy-start(f32[512,1152]{1,0:T(8,128)S(1)} %collective-permute-done.3) | copy-start | bytes 7077892
  191.5 50.7 %collective-permute-start.4 = (f32[512,1152]{1,0:T(8,128)S(1)}, f32[512,1152]{1,0:T(8,128)}, u32[]{:S(2)}, u32[]{:S(2)}) collective-permute-start(f32[512,1152]{1,0:T(8,128)S(1)} %collective-permute-done.3), channel_id=1, source_target_pairs={{126,0},{0,2},{2,4},{4,6},{6,8},{8,10},{10,12},{12,14},{14,16},{16... | collective-permute-start | bytes 7077896 | tf_op jit(solution)/shard_map/ppermute | solution.py:15
  197.7 4.9 copy-start.14
  217.1 50.3 %collective-permute-start.11 = (f32[512,1152]{1,0:T(8,128)S(1)}, f32[512,1152]{1,0:T(8,128)S(1)}, u32[]{:S(2)}, u32[]{:S(2)}) collective-permute-start(f32[512,1152]{1,0:T(8,128)S(1)} %add.239), channel_id=1, source_target_pairs={{126,0},{0,2},{2,4},{4,6},{6,8},{8,10},{10,12},{12,14},{14,16},{16... | collective-permute-start | bytes 7077896 | tf_op jit(solution)/shard_map/ppermute | solution.py:15
  242.2 50.6 %collective-permute-start.5 = (f32[512,1152]{1,0:T(8,128)}, f32[512,1152]{1,0:T(8,128)}, u32[]{:S(2)}, u32[]{:S(2)}) collective-permute-start(f32[512,1152]{1,0:T(8,128)} %collective-permute-done.4), channel_id=1, source_target_pairs={{126,0},{0,2},{2,4},{4,6},{6,8},{8,10},{10,12},{12,14},{14,16},{16... | collective-permute-start | bytes 7077896 | tf_op jit(solution)/shard_map/ppermute | solution.py:15
  250.2 4.9 copy-start.12
  269.0 49.0 %collective-permute-start.12 = (f32[512,1152]{1,0:T(8,128)}, f32[512,1152]{1,0:T(8,128)}, u32[]{:S(2)}, u32[]{:S(2)}) collective-permute-start(f32[512,1152]{1,0:T(8,128)} %add.240), channel_id=1, source_target_pairs={{126,0},{0,2},{2,4},{4,6},{6,8},{8,10},{10,12},{12,14},{14,16},{16... | collective-permute-start | bytes 7077896 | tf_op jit(solution)/shard_map/ppermute | solution.py:15
  291.0 11.2 %copy-start.2 = (f32[1,512,1152]{2,1,0:T(8,128)S(1)}, f32[1,512,1152]{2,1,0:T(8,128)}, u32[]{:S(2)}) copy-start(f32[1,512,1152]{2,1,0:T(8,128)} %param.4) | copy-start | bytes 7077892
  292.8 55.2 %collective-permute-start.6 = (f32[512,1152]{1,0:T(8,128)}, f32[512,1152]{1,0:T(8,128)}, u32[]{:S(2)}, u32[]{:S(2)}) collective-permute-start(f32[512,1152]{1,0:T(8,128)} %collective-permute-done.5), channel_id=1, source_target_pairs={{126,0},{0,2},{2,4},{4,6},{6,8},{8,10},{10,12},{12,14},{14,16},{16... | collective-permute-start | bytes 7077896 | tf_op jit(solution)/shard_map/ppermute | solution.py:15
  301.2 1.0 copy-start.16
  307.1 14.7 %copy-start.5 = (f32[512,1152]{1,0:T(8,128)S(1)}, f32[512,1152]{1,0:T(8,128)}, u32[]{:S(2)}) copy-start(f32[512,1152]{1,0:T(8,128)} %convolution_add_fusion.6) | copy-start | bytes 7077892
  307.1 14.7 %copy-start.7 = (f32[512,1152]{1,0:T(8,128)S(1)}, f32[512,1152]{1,0:T(8,128)}, u32[]{:S(2)}) copy-start(f32[512,1152]{1,0:T(8,128)} %copy-done.6) | copy-start | bytes 7077892
  321.4 47.2 %collective-permute-start.13 = (f32[512,1152]{1,0:T(8,128)}, f32[512,1152]{1,0:T(8,128)}, u32[]{:S(2)}, u32[]{:S(2)}) collective-permute-start(f32[512,1152]{1,0:T(8,128)} %add.241), channel_id=1, source_target_pairs={{126,0},{0,2},{2,4},{4,6},{6,8},{8,10},{10,12},{12,14},{14,16},{16... | collective-permute-start | bytes 7077896 | tf_op jit(solution)/shard_map/ppermute | solution.py:15
  329.9 10.6 %copy-start.15 = (f32[512,512]{1,0:T(8,128)S(1)}, f32[512,512]{1,0:T(8,128)}, u32[]{:S(2)}) copy-start(f32[512,512]{1,0:T(8,128)} %copy-done.14) | copy-start | bytes 3145732
  340.5 7.4 %copy-start.3 = (f32[1,512,1152]{2,1,0:T(8,128)S(1)}, f32[1,512,1152]{2,1,0:T(8,128)}, u32[]{:S(2)}) copy-start(f32[1,512,1152]{2,1,0:T(8,128)} %param.4) | copy-start | bytes 7077892
  355.5 4.9 copy-start.18
  360.4 11.8 %copy-start.13 = (f32[512,512]{1,0:T(8,128)S(1)}, f32[512,512]{1,0:T(8,128)}, u32[]{:S(2)}) copy-start(f32[512,512]{1,0:T(8,128)} %copy-done.12) | copy-start | bytes 3145732
  372.0 13.6 %copy-start.17 = (f32[512,512]{1,0:T(8,128)S(1)}, f32[512,512]{1,0:T(8,128)}, u32[]{:S(2)}) copy-start(f32[512,512]{1,0:T(8,128)} %copy-done.16) | copy-start | bytes 3145732
  372.0 122.7 %collective-permute-start.14 = (f32[512,1152]{1,0:T(8,128)}, f32[512,1152]{1,0:T(8,128)}, u32[]{:S(2)}, u32[]{:S(2)}) collective-permute-start(f32[512,1152]{1,0:T(8,128)} %add.242), channel_id=1, source_target_pairs={{14,0},{16,2},{18,4},{20,6},{22,8},{24,10},{26,12},{28,14},{30,16}... | collective-permute-start | bytes 7077896 | tf_op jit(solution)/shard_map/ppermute | solution.py:15
  484.4 8.5 %copy-start.4 = (f32[1,512,1152]{2,1,0:T(8,128)S(1)}, f32[1,512,1152]{2,1,0:T(8,128)}, u32[]{:S(2)}) copy-start(f32[1,512,1152]{2,1,0:T(8,128)} %param.4) | copy-start | bytes 7077892
where the time goes:
time: 514 us; the launch traced here: 504 us
  waiting for transfers between devices  206 us (40%)
  matrix products  157 us (31%)
  blocking collectives  89 us (17%)
  between operations  23 us (4%)
  other arithmetic  22.3 us (4%)
  starting transfers between devices  5.86 us (1%)
    ppermute x15, waiting for transfers between devices, from_behind(): return lax.ppermute(block, axis, route)  206 us
    psum x1, blocking collectives, shards(): lax.psum((loss_part, cos_part, bias_part), ('blk', 'rep'))  89 us
    dot_general x8, matrix products, shards(): jnp.dot(steepness_weight, arriving_caption_matrix, precision=lax.Precisio...  62.6 us
    dot_general x8, matrix products, shards(): lax.dot_general(picture_unitlength, arriving_caption_matrix, (((1,), (1,)...  54.7 us
    dot_general x8, matrix products, shards(): lax.dot_general(steepness_weight, picture_unitlength, (((0,), (0,)), ((),...  39.3 us
  transfers between devices with their start and end apart: 15, of which 13 were waited for; matrix products, arithmetic and copies ran while one was open for 33% of the time, Pallas kernels for 0%

commit v1 on v0

v1 whole, which is shorter than its diff:
```python
import jax
import jax.numpy as jnp
from jax import lax
from jax.experimental import pallas as pl
from jax.experimental.pallas import tpu as pltpu
from jax.sharding import PartitionSpec as P

MESH = pl.DeviceIdType.MESH
F32 = jnp.float32
BF16 = jnp.bfloat16
EPSILON = 1e-06

N = 512
D = 1152
CHUNKS = 4
R = N // CHUNKS
COLS = [(0, 256), (256, 256), (512, 256), (768, 256), (1024, 128)]

ROW_B, ROW_O, ROW_M, ROW_F = 0, 1024, 1536, 2048
ROWS = 2560
M, B1, B2, B3, C = range(5)
R1, R2, R3, R4, R5 = range(5)
NT = (((1,), (1,)), ((), ()))
NN = (((1,), (0,)), ((), ()))
TN = (((0,), (0,)), ((), ()))


def split(x):
    high = x.astype(BF16)
    return high, (x - high.astype(F32)).astype(BF16)


def dot3(ah, al, bh, bl, dims):
    def one(a, b):
        return lax.dot_general(a, b, dims, preferred_element_type=F32)

    return one(ah, bh) + one(ah, bl) + one(al, bh)


def kernel(
    scale_ref, offset_ref, img, txt,
    out_img, out_txt, out_loss, out_scale, out_offset,
    uih, uil, uth, utl, sh, sl, raw, ret, own, norms, acc, sums, sums_in,
    fs, fr, bs, br, ts, tr, ss, sr, ls,
):
    blk = lax.axis_index("blk")
    rep = lax.axis_index("rep")
    k = blk % 2
    h = (blk // 2) % 2
    m = blk // 4

    def at(dm, hh, kk):
        return (((m + dm + 16) % 16) * 4 + hh * 2 + kk, rep)

    mate = at(0, h, 1 - k)
    after, before = at(1, h, k), at(-1, h, k)
    across = at(0, 1 - h, k)
    diagonal = at(0, 1 - h, 1 - k)
    far = at(2 * k - 1, h, 1 - k)
    odd = at(2 * h - 1, 1 - h, k)
    cube = [(blk + (1 - 2 * ((blk // p) % 2)) * p, rep) for p in (1, 2, 4, 8, 16, 32)] + [(blk, 1 - rep)]

    def remote(src, dst, ssem, rsem, dev):
        return pltpu.make_async_remote_copy(
            src_ref=src, dst_ref=dst, send_sem=ssem, recv_sem=rsem, device_id=dev, device_id_type=MESH
        )

    def rows(i):
        return pl.ds(i * R, R)

    load_img = pltpu.make_async_copy(img, own.at[0], ls.at[0])
    load_txt = pltpu.make_async_copy(txt, own.at[1], ls.at[1])
    load_img.start()
    load_txt.start()

    barrier = pltpu.get_barrier_semaphore()
    partners = [mate, after, before, across, diagonal, far, odd] + cube[2:]
    for dev in partners:
        pl.semaphore_signal(barrier, inc=1, device_id=dev, device_id_type=MESH)
    pl.semaphore_wait(barrier, len(partners))

    def f_text(i):
        return remote(txt.at[rows(i)], raw.at[C, rows(i)], fs.at[0, i], fr.at[C, i], after)

    def f_mate(i):
        return remote(img.at[rows(i)], raw.at[M, rows(i)], fs.at[1, i], fr.at[M, i], mate)

    def f_across(i):
        return remote(img.at[rows(i)], raw.at[B1, rows(i)], fs.at[2, i], fr.at[B1, i], across)

    def f_odd(i):
        return remote(img.at[rows(i)], raw.at[B1, rows(i)], fs.at[2, i], fr.at[B1, i], odd)

    def f_far(i):
        return remote(img.at[rows(i)], raw.at[B3, rows(i)], fs.at[3, i], fr.at[B3, i], far)

    def f_relay(i):
        return remote(raw.at[B3, rows(i)], raw.at[B1, rows(i)], fs.at[4, i], fr.at[B1, i], diagonal)

    def f_pass(i):
        return remote(raw.at[B1, rows(i)], raw.at[B2, rows(i)], fs.at[5, i], fr.at[B2, i], mate)

    h0k1 = (h == 0) & (k == 1)
    for i in range(CHUNKS):
        f_text(i).start()
        pl.when(h == 1)(lambda i=i: f_across(i).start())
        pl.when(h0k1)(lambda i=i: f_odd(i).start())
        pl.when(k == 0)(lambda i=i: f_far(i).start())
        f_mate(i).start()

    scale = jnp.exp(jnp.full((8, 128), scale_ref[0], F32))
    scale11 = scale[0:1, 0:1]
    offset = offset_ref[0]
    acc[...] = jnp.zeros_like(acc)

    def unit(x):
        return x * lax.rsqrt(jnp.sum(x * x, axis=-1, keepdims=True) + EPSILON)

    def put_image(slot, i, row):
        high, low = split(unit(raw[slot, rows(i), :]))
        r = pl.ds(pl.multiple_of(row, R), R)
        uih[r, :] = high
        uil[r, :] = low

    def put_text(i):
        high, low = split(unit(raw[C, rows(i), :]))
        r = pl.ds(N + i * R, R)
        uth[r, :] = high
        utl[r, :] = low

    def slopes(row, n, col, width, home=None):
        r = pl.ds(pl.multiple_of(row, 128), n)
        c = pl.ds(col, width)
        cosine = dot3(uih[r, :], uil[r, :], uth[c, :], utl[c, :], NT)
        z = scale11 * cosine + offset
        if home is not None:
            a = lax.broadcasted_iota(jnp.int32, (n, width), 0) + home
            b = lax.broadcasted_iota(jnp.int32, (n, width), 1)
            sign = jnp.where(a == b, -1.0, 1.0).astype(F32)
            z = sign * z
        e = jnp.exp(z)
        slope = e / (1.0 + e)
        soft = jnp.log1p(e)
        if home is not None:
            slope = sign * slope

        def fold(v):
            v = jnp.sum(v.reshape(n // 8, 8, width), axis=0)
            total = v[:, 0:128]
            for j in range(1, width // 128):
                total = total + v[:, j * 128 : (j + 1) * 128]
            return total

        acc[0:8, :] += fold(soft)
        acc[8:16, :] += fold(slope * cosine)
        acc[16:24, :] += fold(slope)
        high, low = split(scale11 * slope)
        sh[r, c] = high
        sl[r, c] = low

    load_img.wait()
    load_txt.wait()

    @pl.loop(0, CHUNKS)
    def _(i):
        r = pl.ds(pl.multiple_of(i * R, R), R)
        for which in range(2):
            x = own[which, r, :]
            inv = lax.rsqrt(jnp.sum(x * x, axis=-1, keepdims=True) + EPSILON)
            norms[which, r, :] = jnp.broadcast_to(inv, (R, 128))
            high, low = split(x * inv)
            if which == 0:
                q = pl.ds(pl.multiple_of(ROW_O + i * R, R), R)
                uih[q, :] = high
                uil[q, :] = low
            else:
                uth[r, :] = high
                utl[r, :] = low

    @pl.loop(0, 2)
    def _(i):
        slopes(ROW_O + i * 256, 256, 0, 512, home=i * 256)

    for i in range(CHUNKS):
        f_mate(i).wait_recv()
        put_image(M, i, ROW_M + i * R)

    def relay(i):
        @pl.when(h0k1)
        def _():
            f_far(i).wait_recv()
            f_relay(i).start()

    relay(0)

    @pl.when(k == 0)
    def _():
        @pl.loop(0, 2)
        def _(i):
            slopes(ROW_M + i * 256, 256, 0, 512)

    relay(1)

    for i in range(CHUNKS):
        if i + 2 < CHUNKS:
            relay(i + 2)
        f_across(i).wait_recv()
        f_pass(i).start()
        put_image(B1, i, ROW_B + i * 256)
        f_text(i).wait_recv()
        put_text(i)
        f_pass(i).wait_recv()
        put_image(B2, i, ROW_B + i * 256 + R)
        if i < 3:
            slopes(ROW_B + i * 256, 256, 0, 512)
        if i == 1:
            @pl.loop(0, 6)
            def _(j):
                slopes(jnp.where(j < 2, j * 256, ROW_O + (j - 2) * 256), 256, 512, 256)
        if i == 2:
            slopes(ROW_B + 512, 256, 512, 256)

    def g_text(q, d):
        c0, cn = COLS[d]
        cut = (pl.ds(q * 256, 256), pl.ds(c0, cn))
        return remote(raw.at[(C, *cut)], ret.at[(R4, *cut)], ts.at[q * 5 + d], tr.at[q * 5 + d], before)

    def g_pass(j):
        return remote(raw.at[B2, rows(j)], ret.at[R2, rows(j)], bs.at[0, j], br.at[R2, j], mate)

    def g_mate(j):
        return remote(raw.at[M, rows(j)], ret.at[R1, rows(j)], bs.at[1, j], br.at[R1, j], mate)

    def g_across(j):
        return remote(raw.at[B1, rows(j)], ret.at[R3, rows(j)], bs.at[2, j], br.at[R3, j], across)

    def g_odd(j):
        return remote(raw.at[B1, rows(j)], ret.at[R3, rows(j)], bs.at[2, j], br.at[R3, j], odd)

    def g_relay(j):
        return remote(raw.at[B1, rows(j)], ret.at[R5, rows(j)], bs.at[2, j], br.at[R5, j], diagonal)

    def g_far3(j):
        return remote(raw.at[B3, rows(j)], ret.at[R3, rows(j)], bs.at[3, j], br.at[R3, j], far)

    def g_far5(j):
        return remote(raw.at[B3, rows(j)], ret.at[R5, rows(j)], bs.at[3, j], br.at[R5, j], far)

    def image_grad(j):
        f_pass(j).wait_send()
        r = pl.ds(ROW_B + j * 256, 256)
        for c0, cn in COLS:
            c = pl.ds(c0, cn)
            v = dot3(sh[r, :], sl[r, :], uth[:, c], utl[:, c], NN)
            raw[B1, rows(j), c] = v[0:R, :]
            raw[B2, rows(j), c] = v[R:, :]
        g_pass(j).start()

    def image_send(j):
        g_pass(j).wait_recv()
        raw[B1, rows(j), :] += ret[R2, rows(j), :]
        pl.when(h == 0)(lambda: g_across(j).start())
        pl.when((h == 1) & (k == 1))(lambda: g_odd(j).start())
        pl.when((h == 1) & (k == 0))(lambda: g_relay(j).start())

    def text_grad(q, d):
        c0, cn = COLS[d]
        c, t, r = pl.ds(c0, cn), pl.ds(N + q * 256, 256), pl.ds(0, ROW_F)
        raw[C, pl.ds(q * 256, 256), c] = dot3(sh[r, t], sl[r, t], uih[r, c], uil[r, c], TN)

        @pl.when(k == 1)
        def _():
            r = pl.ds(ROW_F, N)
            raw[C, pl.ds(q * 256, 256), c] += dot3(sh[r, t], sl[r, t], uih[r, c], uil[r, c], TN)

        g_text(q, d).start()

    def total(step):
        if step > 0:
            s = step - 1
            remote(sums.at[s], sums_in.at[s], ss.at[s], sr.at[s], cube[s]).wait_recv()
            now = sums[s] + sums_in[s]
        else:
            now = acc[...]
        if step < 7:
            sums[step] = now
            remote(sums.at[step], sums_in.at[step], ss.at[step], sr.at[step], cube[step]).start()
        return now

    slopes(ROW_B, 256, 768, 256)
    image_grad(0)

    slopes(ROW_B + 768, 256, 0, 512)
    slopes(ROW_B + 768, 256, 512, 256)
    image_send(0)

    @pl.when(k == 1)
    def _():
        for i in range(CHUNKS):
            @pl.when(h == 1)
            def _():
                f_far(i).wait_recv()

            put_image(B3, i, ROW_F + i * R)

        @pl.loop(0, 2)
        def _(i):
            slopes(ROW_F + i * 256, 256, 512, 512)

    for d in range(5):
        text_grad(0, d)

    @pl.loop(1, 8)
    def _(j):
        slopes(ROW_B + j * 256, 256, 768, 256)

    image_grad(1)
    total(0)
    text_grad(1, 0)
    image_send(1)
    text_grad(1, 1)
    image_grad(2)
    text_grad(1, 2)
    image_send(2)
    total(1)
    text_grad(1, 3)
    image_grad(3)
    text_grad(1, 4)
    image_send(3)
    total(2)

    @pl.when(k == 1)
    def _():
        for i in range(CHUNKS):
            pl.when(h == 0)(lambda i=i: f_relay(i).wait_send())
        for c0, cn in COLS:
            r, c, t = pl.ds(ROW_F, N), pl.ds(c0, cn), pl.ds(N, N)
            raw[B3, :, c] = dot3(sh[r, t], sl[r, t], uth[t, c], utl[t, c], NN)

        @pl.when(h == 1)
        def _():
            for j in range(CHUNKS):
                g_far5(j).start()

    def far_relay(j):
        @pl.when(h0k1)
        def _():
            g_relay(j).wait_recv()
            raw[B3, rows(j), :] += ret[R5, rows(j), :]
            g_far3(j).start()

    far_relay(0)
    for c0, cn in COLS:
        r, c, t = pl.ds(ROW_M, N), pl.ds(c0, cn), pl.ds(N, N)
        raw[M, :, c] = dot3(sh[r, t], sl[r, t], uth[t, c], utl[t, c], NN)

    @pl.when(k == 0)
    def _():
        for c0, cn in COLS:
            r, c, t = pl.ds(ROW_M, N), pl.ds(c0, cn), pl.ds(0, N)
            raw[M, :, c] += dot3(sh[r, t], sl[r, t], uth[t, c], utl[t, c], NN)

    for j in range(CHUNKS):
        g_mate(j).start()
    total(3)
    far_relay(1)

    for c0, cn in COLS:
        r, c = pl.ds(ROW_O, N), pl.ds(c0, cn)
        own[0, :, c] = dot3(sh[r, :], sl[r, :], uth[:, c], utl[:, c], NN)
    total(4)
    far_relay(2)
    for c0, cn in COLS:
        r, c, t = pl.ds(0, ROW_M), pl.ds(c0, cn), pl.ds(0, N)
        own[1, :, c] = dot3(sh[r, t], sl[r, t], uih[r, c], uil[r, c], TN)

    @pl.when(k == 0)
    def _():
        for c0, cn in COLS:
            r, c, t = pl.ds(ROW_M, N), pl.ds(c0, cn), pl.ds(0, N)
            own[1, :, c] += dot3(sh[r, t], sl[r, t], uih[r, c], uil[r, c], TN)

    total(5)
    far_relay(3)
    total(6)
    final = total(7)

    def whole(v):
        return jnp.sum(jnp.sum(v, axis=0, keepdims=True), axis=1, keepdims=True)

    count = 65536.0
    out_loss[...] = whole(final[0:8, :]) / count
    out_scale[...] = scale11 * whole(final[8:16, :]) / count
    out_offset[...] = whole(final[16:24, :]) / count

    def finish(which, r, n, grad):
        q = pl.ds(ROW_O + r, n)
        u = (uih[q, :].astype(F32) + uil[q, :].astype(F32)) if which == 0 else (
            uth[pl.ds(r, n), :].astype(F32) + utl[pl.ds(r, n), :].astype(F32)
        )
        inv = norms[which, pl.ds(r, n), 0:1]
        along = jnp.sum(u * grad, axis=-1, keepdims=True)
        own[which, pl.ds(r, n), :] = (grad - u * along) * inv

    h1k0 = (h == 1) & (k == 0)

    def store(which, r, n, s):
        dst = (out_img, out_txt)[which]
        return pltpu.make_async_copy(own.at[which, pl.ds(r, n)], dst.at[pl.ds(r, n)], ls.at[s])

    for j in range(CHUNKS):
        g_mate(j).wait_recv()
        g_across(j).wait_recv()

        @pl.when(h1k0)
        def _():
            g_far5(j).wait_recv()
            ret[R3, rows(j), :] += ret[R5, rows(j), :]

        finish(0, j * R, R, own[0, rows(j), :] + ret[R1, rows(j), :] + ret[R3, rows(j), :])
        store(0, j * R, R, j).start()
        if j >= 2:
            q = j - 2
            for d in range(5):
                g_text(q, d).wait_recv()
            for i in range(2):
                r = pl.ds(q * 256 + i * R, R)
                finish(1, q * 256 + i * R, R, own[1, r, :] + ret[R4, r, :])
            store(1, q * 256, 256, 4 + q).start()

    for i in range(CHUNKS):
        f_text(i).wait_send()
        f_mate(i).wait_send()
        pl.when((h == 1) | (k == 1))(lambda i=i: f_across(i).wait_send())
        pl.when(k == 0)(lambda i=i: f_far(i).wait_send())
        g_pass(i).wait_send()
        g_mate(i).wait_send()
        g_across(i).wait_send()
        pl.when(k == 1)(lambda i=i: g_far5(i).wait_send())
    for q in range(2):
        for d in range(5):
            g_text(q, d).wait_send()
    for s in range(7):
        remote(sums.at[s], sums_in.at[s], ss.at[s], sr.at[s], cube[s]).wait_send()
    for j in range(CHUNKS):
        store(0, j * R, R, j).wait()
    for q in range(2):
        store(1, q * 256, 256, 4 + q).wait()


def shards(picture_vectors, caption_vectors, scale_exponent, offset_shift):
    dma = pltpu.SemaphoreType.DMA
    any_space = pl.BlockSpec(memory_space=pl.ANY)
    smem = pl.BlockSpec(memory_space=pltpu.SMEM)
    vmem = pl.BlockSpec(memory_space=pltpu.VMEM)
    block = jax.ShapeDtypeStruct((N, D), F32)
    one = jax.ShapeDtypeStruct((1, 1), F32)
    picture, caption, loss, scale_deriv, offset_deriv = pl.pallas_call(
        kernel,
        out_shape=(block, block, one, one, one),
        in_specs=[smem, smem, any_space, any_space],
        out_specs=(any_space, any_space, vmem, vmem, vmem),
        scratch_shapes=[
            pltpu.VMEM((ROWS, D), BF16),
            pltpu.VMEM((ROWS, D), BF16),
            pltpu.VMEM((2 * N, D), BF16),
            pltpu.VMEM((2 * N, D), BF16),
            pltpu.VMEM((ROWS, 2 * N), BF16),
            pltpu.VMEM((ROWS, 2 * N), BF16),
            pltpu.VMEM((5, N, D), F32),
            pltpu.VMEM((5, N, D), F32),
            pltpu.VMEM((2, N, D), F32),
            pltpu.VMEM((2, N, 128), F32),
            pltpu.VMEM((24, 128), F32),
            pltpu.VMEM((7, 24, 128), F32),
            pltpu.VMEM((7, 24, 128), F32),
            dma((6, CHUNKS)),
            dma((5, CHUNKS)),
            dma((4, CHUNKS)),
            dma((5, CHUNKS)),
            dma((10,)),
            dma((10,)),
            dma((7,)),
            dma((7,)),
            dma((6,)),
        ],
        name="contrastive_window",
        compiler_params=pltpu.CompilerParams(
            collective_id=0, has_side_effects=True, vmem_limit_bytes=63 * 2**20
        ),
    )(
        scale_exponent.reshape(1),
        offset_shift.reshape(1),
        picture_vectors[0],
        caption_vectors[0],
    )
    return (
        picture[None],
        caption[None],
        loss.reshape(()),
        scale_deriv.reshape(()),
        offset_deriv.reshape(()),
    )


def solution(mesh):
    placed = (P("rep", "blk", None), P("rep", "blk", None), P(), P())
    return jax.shard_map(
        shards,
        mesh=mesh,
        in_specs=placed,
        out_specs=(P("rep", "blk", None), P("rep", "blk", None), P(), P(), P()),
        check_vma=False,
    )
```

time: 514 us -> 182 us (0.35)
  the two profiles are of different devices: /device:TPU:0 before, /device:TPU:5 now
where the time goes in v1:
time: 182 us; the launch traced here: 179 us
  Pallas kernels  167 us (92%)
  between operations  7.41 us (4%)
  local copies, waits for them, and re-layouts  4.78 us (3%)
    pallas_call x1, Pallas kernels, shards(): pl.pallas_call(kernel, out_shape=(block, block, one, one, one), in_specs=...  167 us
    unnamed x4, local copies, waits for them, and re-layouts  4.78 us

profile of v1, /device:TPU:5, one launch (start us, length us, event | category | flops | bytes accessed | tf_op | source)
XLA Modules:
  0.0 178.7 jit_solution(18006587764356677851)
XLA Ops:
  1.9 166.5 %contrastive_window.1 = (f32[512,1152]{1,0:T(8,128)}, f32[512,1152]{1,0:T(8,128)}, f32[1,1]{1,0:T(1,128)}, f32[1,1]{1,0:T(1,128)}, f32[1,1]{1,0:T(1,128)}) custom-call(f32[1]{0:T(128)} %bitcast.9.scale_ref, f32[1]{0:T(128)} %bitcast.10.offset_ref, f32[512,1152]{1,0:T(8,128)} %bitcast.11, f32[512,1152]{1,0:T(8,128)} %bitcast.12), custom_call_target="tpu_custom_call" | custom-call | tf_op jit(solution)/shard_map/contrastive_window/pallas_call | solution.py:458
  168.5 0.0 copy-start
  168.5 3.4 %copy.16 = f32[1,512,1152]{2,1,0:T(8,128)} copy(f32[1,512,1152]{2,1,0:T(8,128)} %bitcast.14) | data formatting | bytes 4718592
  171.9 0.0 copy-done
  171.9 1.4 copy.17
Async XLA Ops:
  168.5 3.4 %copy-start = (f32[512,1152]{1,0:T(8,128)S(1)}, f32[512,1152]{1,0:T(8,128)}, u32[]{:S(2)}) copy-start(f32[512,1152]{1,0:T(8,128)} %get-tuple-element.11) | copy-start | bytes 7077892

commit v2 on v1

v2 whole, which is shorter than its diff:
```python
import jax
import jax.numpy as jnp
from jax import lax
from jax.experimental import pallas as pl
from jax.experimental.pallas import tpu as pltpu
from jax.sharding import PartitionSpec as P

MESH = pl.DeviceIdType.MESH
F32 = jnp.float32
BF16 = jnp.bfloat16
EPSILON = 1e-06

N = 512
D = 1152
CHUNKS = 4
R = N // CHUNKS
PIECES = 8
S = N // PIECES

ROW_B, ROW_O, ROW_M, ROW_F = 0, 1024, 1536, 2048
ROWS = 2560
M, B1, B2, B3, C = range(5)
R1, R2, R3, R4, R5 = range(5)
NT = (((1,), (1,)), ((), ()))
NN = (((1,), (0,)), ((), ()))
TN = (((0,), (0,)), ((), ()))


def split(x):
    high = x.astype(BF16)
    return high, (x - high.astype(F32)).astype(BF16)


def dot3(ah, al, bh, bl, dims):
    def one(a, b):
        return lax.dot_general(a, b, dims, preferred_element_type=F32)

    return one(ah, bh) + one(ah, bl) + one(al, bh)


def kernel(
    scale_ref, offset_ref, img, txt,
    out_img, out_txt, out_loss, out_scale, out_offset,
    uih, uil, uth, utl, sh, sl, raw, ret, own, norms, acc, sums, sums_in, group,
    fs, fr, bs, br, ts, tr, ss, sr, gs, gr, ls,
):
    blk = lax.axis_index("blk")
    rep = lax.axis_index("rep")
    k = blk % 2
    h = (blk // 2) % 2
    m = blk // 4

    def at(dm, hh, kk):
        return (((m + dm + 16) % 16) * 4 + hh * 2 + kk, rep)

    mate = at(0, h, 1 - k)
    after, before = at(1, h, k), at(-1, h, k)
    across = at(0, 1 - h, k)
    diagonal = at(0, 1 - h, 1 - k)
    far = at(2 * k - 1, h, 1 - k)
    odd = at(2 * h - 1, 1 - h, k)
    cube = [(blk + (1 - 2 * ((blk // p) % 2)) * p, rep) for p in (1, 16, 32)]
    place = (m % 4) * 4 + h * 2 + rep

    def group_at(o):
        other = (place + o) % 16
        return (m // 4 * 16 + (other // 4) * 4 + ((other // 2) % 2) * 2 + k, other % 2)


    def remote(src, dst, ssem, rsem, dev):
        return pltpu.make_async_remote_copy(
            src_ref=src, dst_ref=dst, send_sem=ssem, recv_sem=rsem, device_id=dev, device_id_type=MESH
        )

    def rows(i):
        return pl.ds(i * R if isinstance(i, int) else pl.multiple_of(i * R, R), R)

    def piece(p):
        return pl.ds(p * S if isinstance(p, int) else pl.multiple_of(p * S, S), S)

    load_img = pltpu.make_async_copy(img, own.at[0], ls.at[0])
    load_txt = pltpu.make_async_copy(txt, own.at[1], ls.at[1])
    load_img.start()
    load_txt.start()

    barrier = pltpu.get_barrier_semaphore()
    partners = [mate, after, before, across, diagonal, far, odd] + cube[1:] + [group_at(o) for o in range(1, 16)]
    for dev in partners:
        pl.semaphore_signal(barrier, inc=1, device_id=dev, device_id_type=MESH)
    pl.semaphore_wait(barrier, len(partners))

    def f_text(i):
        return remote(txt.at[rows(i)], raw.at[C, rows(i)], fs.at[0, i], fr.at[C, i], after)

    def f_mate(i):
        return remote(img.at[rows(i)], raw.at[M, rows(i)], fs.at[1, i], fr.at[M, i], mate)

    def f_across(i):
        return remote(img.at[rows(i)], raw.at[B1, rows(i)], fs.at[2, i], fr.at[B1, i], across)

    def f_odd(i):
        return remote(img.at[rows(i)], raw.at[B1, rows(i)], fs.at[2, i], fr.at[B1, i], odd)

    def f_far(i):
        return remote(img.at[rows(i)], raw.at[B3, rows(i)], fs.at[3, i], fr.at[B3, i], far)

    def f_relay(i):
        return remote(raw.at[B3, rows(i)], raw.at[B1, rows(i)], fs.at[4, i], fr.at[B1, i], diagonal)

    def f_pass(i):
        return remote(raw.at[B1, rows(i)], raw.at[B2, rows(i)], fs.at[5, i], fr.at[B2, i], mate)

    h0k1 = (h == 0) & (k == 1)

    @pl.loop(0, CHUNKS)
    def _(i):
        f_text(i).start()
        pl.when(h == 1)(lambda: f_across(i).start())
        pl.when(h0k1 & (i == 0))(lambda: f_odd(i).start())
        pl.when(k == 0)(lambda: f_far(i).start())
        f_mate(i).start()

    scale = jnp.exp(jnp.full((8, 128), scale_ref[0], F32))
    scale11 = scale[0:1, 0:1]
    offset = offset_ref[0]
    acc[...] = jnp.zeros_like(acc)

    def unit(x):
        return x * lax.rsqrt(jnp.sum(x * x, axis=-1, keepdims=True) + EPSILON)

    def put_image(slot, i, row):
        high, low = split(unit(raw[slot, rows(i), :]))
        r = pl.ds(pl.multiple_of(row, R), R)
        uih[r, :] = high
        uil[r, :] = low

    def put_text(i):
        high, low = split(unit(raw[C, rows(i), :]))
        r = pl.ds(pl.multiple_of(N + i * R, R), R)
        uth[r, :] = high
        utl[r, :] = low

    def slopes(row, n, col, width, home=None):
        r = pl.ds(pl.multiple_of(row, 128), n)
        c = pl.ds(col, width)
        cosine = dot3(uih[r, :], uil[r, :], uth[c, :], utl[c, :], NT)
        z = scale11 * cosine + offset
        if home is not None:
            a = lax.broadcasted_iota(jnp.int32, (n, width), 0) + home
            b = lax.broadcasted_iota(jnp.int32, (n, width), 1)
            sign = jnp.where(a == b, -1.0, 1.0).astype(F32)
            z = sign * z
        e = jnp.exp(z)
        slope = e / (1.0 + e)
        soft = jnp.log1p(e)
        if home is not None:
            slope = sign * slope

        def fold(v):
            v = jnp.sum(v.reshape(n // 8, 8, width), axis=0)
            total = v[:, 0:128]
            for j in range(1, width // 128):
                total = total + v[:, j * 128 : (j + 1) * 128]
            return total

        acc[0:8, :] += fold(soft)
        acc[8:16, :] += fold(slope * cosine)
        acc[16:24, :] += fold(slope)
        high, low = split(scale11 * slope)
        sh[r, c] = high
        sl[r, c] = low

    load_img.wait()
    load_txt.wait()

    @pl.loop(0, CHUNKS)
    def _(i):
        r = pl.ds(pl.multiple_of(i * R, R), R)
        for which in range(2):
            x = own[which, r, :]
            inv = lax.rsqrt(jnp.sum(x * x, axis=-1, keepdims=True) + EPSILON)
            norms[which, r, :] = jnp.broadcast_to(inv, (R, 128))
            high, low = split(x * inv)
            if which == 0:
                q = pl.ds(pl.multiple_of(ROW_O + i * R, R), R)
                uih[q, :] = high
                uil[q, :] = low
            else:
                uth[r, :] = high
                utl[r, :] = low

    @pl.loop(0, 2)
    def _(i):
        slopes(ROW_O + i * 256, 256, 0, 512, home=i * 256)

    @pl.loop(0, CHUNKS)
    def _(i):
        f_mate(i).wait_recv()
        put_image(M, i, ROW_M + i * R)

    def relay(i):
        @pl.when(h0k1)
        def _():
            f_far(i).wait_recv()
            f_relay(i).start()
            pl.when(i + 1 < CHUNKS)(lambda: f_odd(i + 1).start())

    def g_text(q, d, c):
        cut = (pl.ds(q * 256, 256), c)
        return remote(raw.at[(C, *cut)], ret.at[(R4, *cut)], ts.at[q * 5 + d], tr.at[q * 5 + d], before)

    def g_pass(j):
        return remote(raw.at[B2, rows(j)], ret.at[R2, rows(j)], bs.at[0, j], br.at[R2, j], mate)

    def g_mate(j):
        return remote(raw.at[M, rows(j)], ret.at[R1, rows(j)], bs.at[1, j], br.at[R1, j], mate)

    def g_across(p):
        return remote(raw.at[B1, piece(p)], ret.at[R3, piece(p)], bs.at[2, p], br.at[R3, p], across)

    def g_odd(p):
        return remote(raw.at[B1, piece(p)], ret.at[R3, piece(p)], bs.at[2, p], br.at[R3, p], odd)

    def g_relay(p):
        return remote(raw.at[B1, piece(p)], ret.at[R5, piece(p)], bs.at[2, p], br.at[R5, p], diagonal)

    def g_far3(p):
        return remote(raw.at[B3, piece(p)], ret.at[R3, piece(p)], bs.at[3, p], br.at[R3, p], far)

    def g_far5(p):
        return remote(raw.at[B3, piece(p)], ret.at[R5, piece(p)], bs.at[3, p], br.at[R5, p], far)

    def put(dst, value, first):
        if first:
            dst[...] = value
        else:
            dst[...] += value

    def columns(body):
        @pl.loop(0, 4)
        def _(d):
            body(d, pl.ds(pl.multiple_of(d * 256, 256), 256))

        body(4, pl.ds(1024, 128))

    def image_part(dst, row, col, width, first, n=N):
        r, t = pl.ds(row, n), pl.ds(col, width)

        def body(d, c):
            put(dst.at[:, c], dot3(sh[r, t], sl[r, t], uth[t, c], utl[t, c], NN), first)

        columns(body)

    def next_part(j, col, width, first):
        r, t, q = pl.ds(pl.multiple_of(ROW_B + j * 256, 256), 256), pl.ds(col, width), rows(j)

        def body(d, c):
            v = dot3(sh[r, t], sl[r, t], uth[t, c], utl[t, c], NN)
            put(raw.at[B1, q, c], v[0:R, :], first)
            put(raw.at[B2, q, c], v[R:, :], first)

        columns(body)

    def text_part(dst, row, n, col, width, first, then=None):
        r, t = pl.ds(row, n), pl.ds(col, width)

        def body(d, c):
            put(dst.at[:, c], dot3(sh[r, t], sl[r, t], uih[r, c], uil[r, c], TN), first)
            if then is not None:
                then(d, c)

        columns(body)

    first_half, second_half = raw.at[C, pl.ds(0, 256)], raw.at[C, pl.ds(256, 256)]
    HALF0, HALF1 = N, N + 256

    relay(0)

    @pl.when(k == 0)
    def _():
        @pl.loop(0, 2)
        def _(i):
            slopes(ROW_M + i * 256, 256, 0, N)

        image_part(raw.at[M], ROW_M, 0, N, True)

    image_part(own.at[0], ROW_O, 0, N, True)
    relay(1)
    text_part(own.at[1], ROW_O, N, 0, N, True)

    @pl.when(k == 0)
    def _():
        text_part(own.at[1], ROW_M, N, 0, N, False)

    def arrive(i, last=False):
        f_across(i).wait_recv()
        f_pass(i).start()
        put_image(B1, i, ROW_B + i * 256)
        if not last:
            pl.when(i < 2)(lambda: relay(i + 2))
        f_text(i).wait_recv()
        put_text(i)
        f_pass(i).wait_recv()
        put_image(B2, i, ROW_B + i * 256 + R)

    @pl.loop(0, 3)
    def _(i):
        arrive(i)

        @pl.when(i < 2)
        def _():
            slopes(ROW_B + i * 256, 256, 0, 512)
            pl.when(i == 0)(lambda: text_part(own.at[1], ROW_B, 256, 0, N, False))

        @pl.when(i == 1)
        def _():
            @pl.loop(0, 6)
            def _(j):
                slopes(jnp.where(j < 2, j * 256, ROW_O + (j - 2) * 256), 256, HALF0, 256)

            text_part(first_half, ROW_B, 512, HALF0, 256, True)
            text_part(first_half, ROW_O, 1024, HALF0, 256, False)
            f_pass(0).wait_send()
            next_part(0, 0, 768, True)

    slopes(ROW_B + 512, 256, 0, 768)
    text_part(first_half, ROW_B + 512, 256, HALF0, 256, False)

    def next_send(j):
        g_pass(j).wait_recv()
        raw[B1, rows(j), :] += ret[R2, rows(j), :]

        @pl.loop(0, PIECES // CHUNKS)
        def _(e):
            p = j * (PIECES // CHUNKS) + e
            pl.when(h == 0)(lambda: g_across(p).start())
            pl.when((h == 1) & (k == 1))(lambda: g_odd(p).start())
            pl.when((h == 1) & (k == 0))(lambda: g_relay(p).start())

    def total(step):
        if step == 0:
            now = jnp.concatenate(
                [jnp.sum(acc[8 * q : 8 * q + 8, :], axis=0, keepdims=True) for q in range(3)]
                + [jnp.zeros((5, 128), F32)],
                axis=0,
            )
        else:
            s = step - 1
            remote(sums.at[s], sums_in.at[s], ss.at[s], sr.at[s], cube[s]).wait_recv()
            now = sums[s] + sums_in[s]
        if step < 3:
            sums[step] = now
            remote(sums.at[step], sums_in.at[step], ss.at[step], sr.at[step], cube[step]).start()
        else:
            group[place] = now
            for o in range(1, 16):
                share(o).start()

    def share(o):
        return remote(group.at[place], group.at[place], gs.at[o], gr.at[o], group_at(o))

    arrive(3, True)
    slopes(ROW_B, 256, HALF1, 256)
    next_part(0, HALF1, 256, False)
    g_pass(0).start()
    slopes(ROW_B + 256, 256, HALF1, 256)
    next_send(0)
    f_pass(1).wait_send()
    next_part(1, 0, 1024, True)
    g_pass(1).start()
    slopes(ROW_B + 768, 256, 0, 768)
    next_send(1)

    def far_relay(p):
        @pl.when(h0k1)
        def _():
            g_relay(p).wait_recv()
            raw[B3, piece(p), :] += ret[R5, piece(p), :]
            g_far3(p).start()

    @pl.when(k == 1)
    def _():
        @pl.loop(0, CHUNKS)
        def _(i):
            pl.when(h == 1)(lambda: f_far(i).wait_recv())
            put_image(B3, i, ROW_F + i * R)

        @pl.loop(0, 2)
        def _(i):
            slopes(ROW_F + i * 256, 256, N, N)

        text_part(first_half, ROW_F, N, HALF0, 256, False)

    text_part(first_half, ROW_B + 768, 256, HALF0, 256, False, lambda d, c: g_text(0, d, c).start())

    @pl.when(k == 1)
    def _():
        @pl.when(h == 0)
        def _():
            @pl.loop(0, CHUNKS)
            def _(i):
                f_relay(i).wait_send()

        image_part(raw.at[B3], ROW_F, N, N, True)

        @pl.when(h == 1)
        def _():
            @pl.loop(0, PIECES)
            def _(p):
                g_far5(p).start()

    @pl.loop(2, 4)
    def _(j):
        pl.when(j == 2)(lambda: slopes(ROW_B + 512, 256, HALF1, 256))
        f_pass(j).wait_send()
        next_part(j, 0, 1024, True)
        g_pass(j).start()

        @pl.when(j == 2)
        def _():
            @pl.loop(3, 8)
            def _(i):
                slopes(ROW_B + i * 256, 256, HALF1, 256)

            far_relay(0)
            far_relay(1)
            next_send(2)
            total(0)
            text_part(second_half, 0, 1024, HALF1, 256, True)

            @pl.when(k == 1)
            def _():
                text_part(second_half, ROW_F, N, HALF1, 256, False)

            total(1)
            text_part(second_half, ROW_O, 1024, HALF1, 256, False, lambda d, c: g_text(1, d, c).start())
            far_relay(2)
            far_relay(3)

    total(2)
    next_send(3)

    @pl.when(k == 0)
    def _():
        image_part(raw.at[M], ROW_M, N, N, False)

    @pl.when(k == 1)
    def _():
        image_part(raw.at[M], ROW_M, N, N, True)

    @pl.loop(0, CHUNKS)
    def _(j):
        g_mate(j).start()

    far_relay(4)
    total(3)

    image_part(own.at[0], ROW_O, N, N, False)
    far_relay(5)
    text_part(own.at[1], ROW_B + 256, 768, 0, N, False)

    def whole(v):
        return jnp.sum(jnp.sum(v, axis=0, keepdims=True), axis=1, keepdims=True)

    def finish(which, r, n, grad):
        r = pl.multiple_of(r, n)
        high, low, q = (uih, uil, pl.ds(pl.multiple_of(ROW_O + r, n), n)) if which == 0 else (uth, utl, pl.ds(r, n))
        u = high[q, :].astype(F32) + low[q, :].astype(F32)
        inv = norms[which, pl.ds(r, n), 0:1]
        along = jnp.sum(u * grad, axis=-1, keepdims=True)
        own[which, pl.ds(r, n), :] = (grad - u * along) * inv

    h1k0 = (h == 1) & (k == 0)

    def store(which, r, n, s):
        dst = (out_img, out_txt)[which]
        r = pl.multiple_of(r, n)
        return pltpu.make_async_copy(own.at[which, pl.ds(r, n)], dst.at[pl.ds(r, n)], ls.at[s])

    @pl.loop(0, PIECES)
    def _(p):
        pl.when(p < 2)(lambda: far_relay(p + 6))
        pl.when(p % 2 == 0)(lambda: g_mate(p // 2).wait_recv())
        g_across(p).wait_recv()

        @pl.when(h1k0)
        def _():
            g_far5(p).wait_recv()
            ret[R3, piece(p), :] += ret[R5, piece(p), :]

        finish(0, p * S, S, own[0, piece(p), :] + ret[R1, piece(p), :] + ret[R3, piece(p), :])
        store(0, p * S, S, p).start()

        @pl.when(p % 4 == 2)
        def _():
            q = p // 4
            columns(lambda d, c: g_text(q, d, c).wait_recv())

            @pl.loop(0, 2)
            def _(i):
                start = pl.multiple_of(q * 256 + i * R, R)
                r = pl.ds(start, R)
                finish(1, start, R, own[1, r, :] + ret[R4, r, :])

            store(1, pl.multiple_of(q * 256, 256), 256, PIECES + q).start()

    for o in range(1, 16):
        share(o).wait_recv()
    final = group[0]
    for o in range(1, 16):
        final = final + group[o]

    count = 65536.0
    out_loss[...] = whole(final[0:1, :]) / count
    out_scale[...] = scale11 * whole(final[1:2, :]) / count
    out_offset[...] = whole(final[2:3, :]) / count

    @pl.loop(0, CHUNKS)
    def _(i):
        f_text(i).wait_send()
        f_mate(i).wait_send()
        pl.when((h == 1) | (k == 1))(lambda: f_across(i).wait_send())
        pl.when(k == 0)(lambda: f_far(i).wait_send())
        g_pass(i).wait_send()
        g_mate(i).wait_send()

    @pl.loop(0, PIECES)
    def _(p):
        g_across(p).wait_send()
        pl.when(k == 1)(lambda: g_far5(p).wait_send())
        store(0, p * S, S, p).wait()

    for q in range(2):
        columns(lambda d, c, q=q: g_text(q, d, c).wait_send())
        store(1, q * 256, 256, PIECES + q).wait()
    for s in range(3):
        remote(sums.at[s], sums_in.at[s], ss.at[s], sr.at[s], cube[s]).wait_send()
    for o in range(1, 16):
        share(o).wait_send()


def shards(picture_vectors, caption_vectors, scale_exponent, offset_shift):
    dma = pltpu.SemaphoreType.DMA
    any_space = pl.BlockSpec(memory_space=pl.ANY)
    smem = pl.BlockSpec(memory_space=pltpu.SMEM)
    vmem = pl.BlockSpec(memory_space=pltpu.VMEM)
    block = jax.ShapeDtypeStruct((N, D), F32)
    one = jax.ShapeDtypeStruct((1, 1), F32)
    picture, caption, loss, scale_deriv, offset_deriv = pl.pallas_call(
        kernel,
        out_shape=(block, block, one, one, one),
        in_specs=[smem, smem, any_space, any_space],
        out_specs=(any_space, any_space, vmem, vmem, vmem),
        scratch_shapes=[
            pltpu.VMEM((ROWS, D), BF16),
            pltpu.VMEM((ROWS, D), BF16),
            pltpu.VMEM((2 * N, D), BF16),
            pltpu.VMEM((2 * N, D), BF16),
            pltpu.VMEM((ROWS, 2 * N), BF16),
            pltpu.VMEM((ROWS, 2 * N), BF16),
            pltpu.VMEM((5, N, D), F32),
            pltpu.VMEM((5, N, D), F32),
            pltpu.VMEM((2, N, D), F32),
            pltpu.VMEM((2, N, 128), F32),
            pltpu.VMEM((24, 128), F32),
            pltpu.VMEM((3, 8, 128), F32),
            pltpu.VMEM((3, 8, 128), F32),
            pltpu.VMEM((16, 8, 128), F32),
            dma((6, CHUNKS)),
            dma((5, CHUNKS)),
            dma((4, PIECES)),
            dma((5, PIECES)),
            dma((10,)),
            dma((10,)),
            dma((3,)),
            dma((3,)),
            dma((16,)),
            dma((16,)),
            dma((PIECES + 2,)),
        ],
        name="contrastive_window",
        compiler_params=pltpu.CompilerParams(
            collective_id=0, has_side_effects=True, vmem_limit_bytes=63 * 2**20
        ),
    )(
        scale_exponent.reshape(1),
        offset_shift.reshape(1),
        picture_vectors[0],
        caption_vectors[0],
    )
    return (
        picture[None],
        caption[None],
        loss.reshape(()),
        scale_deriv.reshape(()),
        offset_deriv.reshape(()),
    )


def solution(mesh):
    placed = (P("rep", "blk", None), P("rep", "blk", None), P(), P())
    return jax.shard_map(
        shards,
        mesh=mesh,
        in_specs=placed,
        out_specs=(P("rep", "blk", None), P("rep", "blk", None), P(), P(), P()),
        check_vma=False,
    )
```

time: 182 us -> 156 us (0.86)
  the two profiles are of different devices: /device:TPU:5 before, /device:TPU:40 now
where the time goes in v2:
time: 156 us
  Pallas kernels  144 us (92%)
  between operations  7.19 us (5%)
  local copies, waits for them, and re-layouts  4.78 us (3%)
    pallas_call x1, Pallas kernels, shards(): pl.pallas_call(kernel, out_shape=(block, block, one, one, one), in_specs=...  144 us
    unnamed x4, local copies, waits for them, and re-layouts  4.78 us

profile of v2, /device:TPU:40, one launch (start us, length us, event | category | flops | bytes accessed | tf_op | source)
XLA Modules:
  0.0 156.3 jit_solution(2283419909527727243)
XLA Ops:
  1.9 144.3 %contrastive_window.1 = (f32[512,1152]{1,0:T(8,128)}, f32[512,1152]{1,0:T(8,128)}, f32[1,1]{1,0:T(1,128)}, f32[1,1]{1,0:T(1,128)}, f32[1,1]{1,0:T(1,128)}) custom-call(f32[1]{0:T(128)} %bitcast.9.scale_ref, f32[1]{0:T(128)} %bitcast.10.offset_ref, f32[512,1152]{1,0:T(8,128)} %bitcast.11, f32[512,1152]{1,0:T(8,128)} %bitcast.12), custom_call_target="tpu_custom_call" | custom-call | tf_op jit(solution)/shard_map/contrastive_window/pallas_call | solution.py:549
  146.3 0.0 copy-start
  146.3 3.4 %copy.16 = f32[1,512,1152]{2,1,0:T(8,128)} copy(f32[1,512,1152]{2,1,0:T(8,128)} %bitcast.14) | data formatting | bytes 4718592
  149.6 0.0 copy-done
  149.6 1.4 copy.17
Async XLA Ops:
  146.3 3.4 %copy-start = (f32[512,1152]{1,0:T(8,128)S(1)}, f32[512,1152]{1,0:T(8,128)}, u32[]{:S(2)}) copy-start(f32[512,1152]{1,0:T(8,128)} %get-tuple-element.11) | copy-start | bytes 7077892

commit v3 on v2

--- a/solution.py
+++ b/solution.py
@@ -41,8 +41,8 @@
 def kernel(
     scale_ref, offset_ref, img, txt,
     out_img, out_txt, out_loss, out_scale, out_offset,
-    uih, uil, uth, utl, sh, sl, raw, ret, own, norms, acc, sums, sums_in, group,
-    fs, fr, bs, br, ts, tr, ss, sr, gs, gr, ls,
+    uih, uil, uth, utl, sh, sl, raw, ret, own, norms, acc, column, group, given, sums,
+    fs, fr, bs, br, ts, tr, cs, cr, gs, gr, ls, vs,
 ):
     blk = lax.axis_index("blk")
     rep = lax.axis_index("rep")
@@ -59,7 +59,12 @@
     diagonal = at(0, 1 - h, 1 - k)
     far = at(2 * k - 1, h, 1 - k)
     odd = at(2 * h - 1, 1 - h, k)
-    cube = [(blk + (1 - 2 * ((blk // p) % 2)) * p, rep) for p in (1, 16, 32)]
+    level = (m // 4) * 2 + k
+
+    def column_at(o):
+        other = (level + o) % 8
+        return ((other // 2) * 16 + (m % 4) * 4 + h * 2 + other % 2, rep)
+
     place = (m % 4) * 4 + h * 2 + rep
 
     def group_at(o):
@@ -82,9 +87,14 @@
     load_txt = pltpu.make_async_copy(txt, own.at[1], ls.at[1])
     load_img.start()
     load_txt.start()
+    load_scale = pltpu.make_async_copy(scale_ref, given.at[0], vs.at[0])
+    load_offset = pltpu.make_async_copy(offset_ref, given.at[1], vs.at[1])
+    load_scale.start()
+    load_offset.start()
 
     barrier = pltpu.get_barrier_semaphore()
-    partners = [mate, after, before, across, diagonal, far, odd] + cube[1:] + [group_at(o) for o in range(1, 16)]
+    partners = [mate, after, before, across, diagonal, far, odd]
+    partners += [column_at(o) for o in range(1, 8)] + [group_at(o) for o in range(1, 16)]
     for dev in partners:
         pl.semaphore_signal(barrier, inc=1, device_id=dev, device_id_type=MESH)
     pl.semaphore_wait(barrier, len(partners))
@@ -120,9 +130,10 @@
         pl.when(k == 0)(lambda: f_far(i).start())
         f_mate(i).start()
 
-    scale = jnp.exp(jnp.full((8, 128), scale_ref[0], F32))
-    scale11 = scale[0:1, 0:1]
-    offset = offset_ref[0]
+    load_scale.wait()
+    load_offset.wait()
+    scale11 = jnp.exp(given[0])
+    offset = given[1]
     acc[...] = jnp.zeros_like(acc)
 
     def unit(x):
@@ -292,12 +303,11 @@
     def _():
         text_part(own.at[1], ROW_M, N, 0, N, False)
 
-    def arrive(i, last=False):
+    def arrive(i):
         f_across(i).wait_recv()
         f_pass(i).start()
         put_image(B1, i, ROW_B + i * 256)
-        if not last:
-            pl.when(i < 2)(lambda: relay(i + 2))
+        pl.when(i < 2)(lambda: relay(i + 2))
         f_text(i).wait_recv()
         put_text(i)
         f_pass(i).wait_recv()
@@ -334,42 +344,59 @@
         def _(e):
             p = j * (PIECES // CHUNKS) + e
             pl.when(h == 0)(lambda: g_across(p).start())
-            pl.when((h == 1) & (k == 1))(lambda: g_odd(p).start())
             pl.when((h == 1) & (k == 0))(lambda: g_relay(p).start())
 
-    def total(step):
-        if step == 0:
-            now = jnp.concatenate(
-                [jnp.sum(acc[8 * q : 8 * q + 8, :], axis=0, keepdims=True) for q in range(3)]
-                + [jnp.zeros((5, 128), F32)],
-                axis=0,
-            )
-        else:
-            s = step - 1
-            remote(sums.at[s], sums_in.at[s], ss.at[s], sr.at[s], cube[s]).wait_recv()
-            now = sums[s] + sums_in[s]
-        if step < 3:
-            sums[step] = now
-            remote(sums.at[step], sums_in.at[step], ss.at[step], sr.at[step], cube[step]).start()
-        else:
-            group[place] = now
-            for o in range(1, 16):
-                share(o).start()
+    def odd_send(j):
+        @pl.when((h == 1) & (k == 1))
+        def _():
+            @pl.loop(0, PIECES // CHUNKS)
+            def _(e):
+                g_odd(j * (PIECES // CHUNKS) + e).start()
+
+    def column_share(o):
+        return remote(column.at[level], column.at[level], cs.at[o], cr.at[o], column_at(o))
 
     def share(o):
         return remote(group.at[place], group.at[place], gs.at[o], gr.at[o], group_at(o))
 
-    arrive(3, True)
+    def share_column():
+        column[level] = jnp.concatenate(
+            [jnp.sum(acc[8 * q : 8 * q + 8, :], axis=0, keepdims=True) for q in range(3)]
+            + [jnp.zeros((5, 128), F32)],
+            axis=0,
+        )
+        for o in range(1, 8):
+            column_share(o).start()
+
+    def share_group():
+        for o in range(1, 8):
+            column_share(o).wait_recv()
+        now = column[0]
+        for o in range(1, 8):
+            now = now + column[o]
+        group[place] = now
+        for o in range(1, 16):
+            share(o).start()
+
+    f_text(3).wait_recv()
+    put_text(3)
     slopes(ROW_B, 256, HALF1, 256)
     next_part(0, HALF1, 256, False)
     g_pass(0).start()
+    f_across(3).wait_recv()
+    f_pass(3).start()
+    put_image(B1, 3, ROW_B + 768)
     slopes(ROW_B + 256, 256, HALF1, 256)
     next_send(0)
+    odd_send(0)
+    f_pass(3).wait_recv()
+    put_image(B2, 3, ROW_B + 768 + R)
     f_pass(1).wait_send()
     next_part(1, 0, 1024, True)
     g_pass(1).start()
     slopes(ROW_B + 768, 256, 0, 768)
     next_send(1)
+    odd_send(1)
 
     def far_relay(p):
         @pl.when(h0k1)
@@ -409,6 +436,9 @@
             def _(p):
                 g_far5(p).start()
 
+    far_relay(0)
+    far_relay(1)
+
     @pl.loop(2, 4)
     def _(j):
         pl.when(j == 2)(lambda: slopes(ROW_B + 512, 256, HALF1, 256))
@@ -422,22 +452,20 @@
             def _(i):
                 slopes(ROW_B + i * 256, 256, HALF1, 256)
 
-            far_relay(0)
-            far_relay(1)
+            share_column()
+            far_relay(2)
             next_send(2)
-            total(0)
             text_part(second_half, 0, 1024, HALF1, 256, True)
+            odd_send(2)
+            far_relay(3)
 
             @pl.when(k == 1)
             def _():
                 text_part(second_half, ROW_F, N, HALF1, 256, False)
 
-            total(1)
             text_part(second_half, ROW_O, 1024, HALF1, 256, False, lambda d, c: g_text(1, d, c).start())
-            far_relay(2)
-            far_relay(3)
-
-    total(2)
+            far_relay(4)
+
     next_send(3)
 
     @pl.when(k == 0)
@@ -452,12 +480,13 @@
     def _(j):
         g_mate(j).start()
 
-    far_relay(4)
-    total(3)
+    far_relay(5)
 
     image_part(own.at[0], ROW_O, N, N, False)
-    far_relay(5)
+    odd_send(3)
     text_part(own.at[1], ROW_B + 256, 768, 0, N, False)
+
+    share_group()
 
     def whole(v):
         return jnp.sum(jnp.sum(v, axis=0, keepdims=True), axis=1, keepdims=True)
@@ -511,9 +540,15 @@
         final = final + group[o]
 
     count = 65536.0
-    out_loss[...] = whole(final[0:1, :]) / count
-    out_scale[...] = scale11 * whole(final[1:2, :]) / count
-    out_offset[...] = whole(final[2:3, :]) / count
+    sums[0] = whole(final[0:1, :]) / count
+    sums[1] = scale11 * whole(final[1:2, :]) / count
+    sums[2] = whole(final[2:3, :]) / count
+    give_sums = [
+        pltpu.make_async_copy(sums.at[q], dst, vs.at[2 + q])
+        for q, dst in enumerate((out_loss, out_scale, out_offset))
+    ]
+    for give in give_sums:
+        give.start()
 
     @pl.loop(0, CHUNKS)
     def _(i):
@@ -533,24 +568,42 @@
     for q in range(2):
         columns(lambda d, c, q=q: g_text(q, d, c).wait_send())
         store(1, q * 256, 256, PIECES + q).wait()
-    for s in range(3):
-        remote(sums.at[s], sums_in.at[s], ss.at[s], sr.at[s], cube[s]).wait_send()
+    for o in range(1, 8):
+        column_share(o).wait_send()
     for o in range(1, 16):
         share(o).wait_send()
+    for give in give_sums:
+        give.wait()
+
+
+def hand_over(a, b, c, d, e, oa, ob, oc, od, oe, held, held_c, held_d, held_e, sem):
+    def steps(src, here, dst, s):
+        return pltpu.make_async_copy(src, here, sem.at[0, s]), pltpu.make_async_copy(here, dst, sem.at[1, s])
+
+    order = [steps(c, held_c, oc, 0), steps(d, held_d, od, 1), steps(e, held_e, oe, 2)]
+    for i in range(CHUNKS):
+        r = pl.ds(i * R, R)
+        order.append(steps(a.at[r], held.at[0, r], oa.at[r], 3 + 2 * i))
+        order.append(steps(b.at[r], held.at[1, r], ob.at[r], 4 + 2 * i))
+    for fetch, _ in order:
+        fetch.start()
+    for fetch, give in order:
+        fetch.wait()
+        give.start()
+    for _, give in order:
+        give.wait()
 
 
 def shards(picture_vectors, caption_vectors, scale_exponent, offset_shift):
     dma = pltpu.SemaphoreType.DMA
     any_space = pl.BlockSpec(memory_space=pl.ANY)
-    smem = pl.BlockSpec(memory_space=pltpu.SMEM)
-    vmem = pl.BlockSpec(memory_space=pltpu.VMEM)
     block = jax.ShapeDtypeStruct((N, D), F32)
     one = jax.ShapeDtypeStruct((1, 1), F32)
     picture, caption, loss, scale_deriv, offset_deriv = pl.pallas_call(
         kernel,
         out_shape=(block, block, one, one, one),
-        in_specs=[smem, smem, any_space, any_space],
-        out_specs=(any_space, any_space, vmem, vmem, vmem),
+        in_specs=[any_space] * 4,
+        out_specs=(any_space,) * 5,
         scratch_shapes=[
             pltpu.VMEM((ROWS, D), BF16),
             pltpu.VMEM((ROWS, D), BF16),
@@ -563,31 +616,41 @@
             pltpu.VMEM((2, N, D), F32),
             pltpu.VMEM((2, N, 128), F32),
             pltpu.VMEM((24, 128), F32),
-            pltpu.VMEM((3, 8, 128), F32),
-            pltpu.VMEM((3, 8, 128), F32),
+            pltpu.VMEM((8, 8, 128), F32),
             pltpu.VMEM((16, 8, 128), F32),
+            pltpu.VMEM((2, 1, 1), F32),
+            pltpu.VMEM((3, 1, 1), F32),
             dma((6, CHUNKS)),
             dma((5, CHUNKS)),
             dma((4, PIECES)),
             dma((5, PIECES)),
             dma((10,)),
             dma((10,)),
-            dma((3,)),
-            dma((3,)),
+            dma((8,)),
+            dma((8,)),
             dma((16,)),
             dma((16,)),
             dma((PIECES + 2,)),
+            dma((5,)),
         ],
         name="contrastive_window",
         compiler_params=pltpu.CompilerParams(
             collective_id=0, has_side_effects=True, vmem_limit_bytes=63 * 2**20
         ),
     )(
-        scale_exponent.reshape(1),
-        offset_shift.reshape(1),
+        scale_exponent.reshape(1, 1),
+        offset_shift.reshape(1, 1),
         picture_vectors[0],
         caption_vectors[0],
     )
+    picture, caption, loss, scale_deriv, offset_deriv = pl.pallas_call(
+        hand_over,
+        out_shape=(block, block, one, one, one),
+        in_specs=[any_space] * 5,
+        out_specs=(any_space,) * 5,
+        scratch_shapes=[pltpu.VMEM((2, N, D), F32)] + [pltpu.VMEM((1, 1), F32)] * 3 + [dma((2, 3 + 2 * CHUNKS))],
+        name="hand_over",
+    )(picture, caption, loss, scale_deriv, offset_deriv)
     return (
         picture[None],
         caption[None],

time: 156 us -> 141 us (0.904)
  the two profiles are of different devices: /device:TPU:40 before, /device:TPU:0 now
where the time goes in v3:
time: 141 us
  Pallas kernels  139 us (99%)
  between operations  2.13 us (2%)
    pallas_call x1, Pallas kernels, shards(): pl.pallas_call(kernel, out_shape=(block, block, one, one, one), in_specs=...  133 us
    pallas_call x1, Pallas kernels, shards(): pl.pallas_call(hand_over, out_shape=(block, block, one, one, one), in_spe...  6.04 us

profile of v3, /device:TPU:0, one launch (start us, length us, event | category | flops | bytes accessed | tf_op | source)
XLA Modules:
  0.0 141.1 jit_solution(7940363681927374297)
XLA Ops:
  1.9 133.0 %contrastive_window.1 = (f32[512,1152]{1,0:T(8,128)}, f32[512,1152]{1,0:T(8,128)}, f32[1,1]{1,0:T(1,128)}, f32[1,1]{1,0:T(1,128)}, f32[1,1]{1,0:T(1,128)}) custom-call(f32[1,1]{1,0:T(1,128)} %bitcast.9.scale_ref, f32[1,1]{1,0:T(1,128)} %bitcast.10.offset_ref, f32[512,1152]{1,0:T(8,128)} %bitcast.11, f32[512,1152]{1,0:T(8,128)} %bitcast.12), custom_call_target="tpu_custom_call" | custom-call | tf_op jit(solution)/shard_map/contrastive_window/pallas_call | solution.py:602
  134.9 6.0 %hand_over.1 = (f32[512,1152]{1,0:T(8,128)}, f32[512,1152]{1,0:T(8,128)}, f32[1,1]{1,0:T(1,128)}, f32[1,1]{1,0:T(1,128)}, f32[1,1]{1,0:T(1,128)}) custom-call(f32[512,1152]{1,0:T(8,128)} %get-tuple-element.15.a, f32[512,1152]{1,0:T(8,128)} %get-tuple-element.16.b, f32[1,1]{1,0:T(1,128)} %get-tuple-element.17.c, f32[1,1]{1,0:T(1,128)} %get-tuple-element.18.d, ...), custom_call_target="tpu_custom_call" | custom-call | tf_op jit(solution)/shard_map/hand_over/pallas_call | solution.py:646

commit v4 on v3

--- a/solution.py
+++ b/solution.py
@@ -16,6 +16,7 @@
 R = N // CHUNKS
 PIECES = 8
 S = N // PIECES
+TURN = 6
 
 ROW_B, ROW_O, ROW_M, ROW_F = 0, 1024, 1536, 2048
 ROWS = 2560
@@ -121,6 +122,7 @@
         return remote(raw.at[B1, rows(i)], raw.at[B2, rows(i)], fs.at[5, i], fr.at[B2, i], mate)
 
     h0k1 = (h == 0) & (k == 1)
+    h1k1 = (h == 1) & (k == 1)
 
     @pl.loop(0, CHUNKS)
     def _(i):
@@ -152,6 +154,14 @@
         utl[r, :] = low
 
     def slopes(row, n, col, width, home=None):
+        if width == 256:
+            return tile(row, n, col, width, home)
+
+        @pl.loop(0, width // 256)
+        def _(j):
+            tile(row, n, pl.multiple_of(col + j * 256, 256), 256, None if home is None else home - j * 256)
+
+    def tile(row, n, col, width, home):
         r = pl.ds(pl.multiple_of(row, 128), n)
         c = pl.ds(col, width)
         cosine = dot3(uih[r, :], uil[r, :], uth[c, :], utl[c, :], NT)
@@ -218,7 +228,7 @@
 
     def g_text(q, d, c):
         cut = (pl.ds(q * 256, 256), c)
-        return remote(raw.at[(C, *cut)], ret.at[(R4, *cut)], ts.at[q * 5 + d], tr.at[q * 5 + d], before)
+        return remote(raw.at[(C, *cut)], ret.at[(R4, *cut)], ts.at[q * 3 + d], tr.at[q * 3 + d], before)
 
     def g_pass(j):
         return remote(raw.at[B2, rows(j)], ret.at[R2, rows(j)], bs.at[0, j], br.at[R2, j], mate)
@@ -231,6 +241,12 @@
 
     def g_odd(p):
         return remote(raw.at[B1, piece(p)], ret.at[R3, piece(p)], bs.at[2, p], br.at[R3, p], odd)
+
+    def g_ahead(p):
+        return remote(raw.at[B1, piece(p)], ret.at[R5, piece(p)], bs.at[2, p], br.at[R5, p], after)
+
+    def g_turn(p):
+        return remote(ret.at[R5, piece(p)], ret.at[R3, piece(p)], bs.at[4, p], br.at[R3, p], across)
 
     def g_relay(p):
         return remote(raw.at[B1, piece(p)], ret.at[R5, piece(p)], bs.at[2, p], br.at[R5, p], diagonal)
@@ -248,11 +264,11 @@
             dst[...] += value
 
     def columns(body):
-        @pl.loop(0, 4)
+        @pl.loop(0, 2)
         def _(d):
-            body(d, pl.ds(pl.multiple_of(d * 256, 256), 256))
-
-        body(4, pl.ds(1024, 128))
+            body(d, pl.ds(pl.multiple_of(d * 512, 512), 512))
+
+        body(2, pl.ds(1024, 128))
 
     def image_part(dst, row, col, width, first, n=N):
         r, t = pl.ds(row, n), pl.ds(col, width)
@@ -336,22 +352,45 @@
     slopes(ROW_B + 512, 256, 0, 768)
     text_part(first_half, ROW_B + 512, 256, HALF0, 256, False)
 
-    def next_send(j):
+    def next_add(j):
         g_pass(j).wait_recv()
         raw[B1, rows(j), :] += ret[R2, rows(j), :]
 
+    def pieces_of(j, body):
         @pl.loop(0, PIECES // CHUNKS)
         def _(e):
-            p = j * (PIECES // CHUNKS) + e
-            pl.when(h == 0)(lambda: g_across(p).start())
-            pl.when((h == 1) & (k == 0))(lambda: g_relay(p).start())
+            body(j * (PIECES // CHUNKS) + e)
+
+    def relayed_send(j):
+        pl.when((h == 1) & (k == 0))(lambda: pieces_of(j, lambda p: g_relay(p).start()))
+
+    def across_send(j):
+        pl.when(h == 0)(lambda: pieces_of(j, lambda p: g_across(p).start()))
 
     def odd_send(j):
-        @pl.when((h == 1) & (k == 1))
-        def _():
-            @pl.loop(0, PIECES // CHUNKS)
-            def _(e):
-                g_odd(j * (PIECES // CHUNKS) + e).start()
+        pl.when(h1k1)(lambda: pieces_of(j, odd_piece))
+
+    def odd_piece(p):
+        pl.when(p < TURN)(lambda: g_odd(p).start())
+        pl.when(p >= TURN)(lambda: g_ahead(p).start())
+
+    def odd_relay(p):
+        @pl.when(h1k1)
+        def _():
+            g_ahead(p).wait_recv()
+            g_turn(p).start()
+
+    def next_send(j):
+        next_add(j)
+        relayed_send(j)
+        across_send(j)
+
+    def far_send(first, last):
+        @pl.when(h1k1)
+        def _():
+            @pl.loop(first, last)
+            def _(p):
+                g_far5(p).start()
 
     def column_share(o):
         return remote(column.at[level], column.at[level], cs.at[o], cr.at[o], column_at(o))
@@ -377,6 +416,21 @@
         group[place] = now
         for o in range(1, 16):
             share(o).start()
+
+    def far_relay(p):
+        @pl.when(h0k1)
+        def _():
+            g_relay(p).wait_recv()
+            raw[B3, piece(p), :] += ret[R5, piece(p), :]
+            g_far3(p).start()
+
+    def first_send():
+        text_part(first_half, ROW_B + 768, 256, HALF0, 256, False, lambda d, c: g_text(0, d, c).start())
+
+    def next_full(j):
+        f_pass(j).wait_send()
+        next_part(j, 0, 1024, True)
+        g_pass(j).start()
 
     f_text(3).wait_recv()
     put_text(3)
@@ -391,19 +445,11 @@
     odd_send(0)
     f_pass(3).wait_recv()
     put_image(B2, 3, ROW_B + 768 + R)
-    f_pass(1).wait_send()
-    next_part(1, 0, 1024, True)
-    g_pass(1).start()
     slopes(ROW_B + 768, 256, 0, 768)
+    pl.when(k == 0)(first_send)
+    next_full(1)
     next_send(1)
     odd_send(1)
-
-    def far_relay(p):
-        @pl.when(h0k1)
-        def _():
-            g_relay(p).wait_recv()
-            raw[B3, piece(p), :] += ret[R5, piece(p), :]
-            g_far3(p).start()
 
     @pl.when(k == 1)
     def _():
@@ -417,11 +463,8 @@
             slopes(ROW_F + i * 256, 256, N, N)
 
         text_part(first_half, ROW_F, N, HALF0, 256, False)
-
-    text_part(first_half, ROW_B + 768, 256, HALF0, 256, False, lambda d, c: g_text(0, d, c).start())
-
-    @pl.when(k == 1)
-    def _():
+        first_send()
+
         @pl.when(h == 0)
         def _():
             @pl.loop(0, CHUNKS)
@@ -430,43 +473,57 @@
 
         image_part(raw.at[B3], ROW_F, N, N, True)
 
-        @pl.when(h == 1)
-        def _():
-            @pl.loop(0, PIECES)
-            def _(p):
-                g_far5(p).start()
-
-    far_relay(0)
-    far_relay(1)
-
-    @pl.loop(2, 4)
-    def _(j):
-        pl.when(j == 2)(lambda: slopes(ROW_B + 512, 256, HALF1, 256))
-        f_pass(j).wait_send()
-        next_part(j, 0, 1024, True)
-        g_pass(j).start()
-
-        @pl.when(j == 2)
-        def _():
-            @pl.loop(3, 8)
+    far_send(0, 3)
+    for p in range(2):
+        far_relay(p)
+
+    slopes(ROW_B + 512, 256, HALF1, 256)
+    next_full(2)
+    slopes(ROW_B + 768, 256, HALF1, 256)
+
+    @pl.loop(0, 5)
+    def _(step):
+        def job(on0, on1):
+            return pl.when(((k == 0) & (step == on0)) | ((k == 1) & (step == on1)))
+
+        @job(2, 0)
+        def _():
+            next_send(2)
+            odd_send(2)
+
+        @job(3, 1)
+        def _():
+            next_full(3)
+            far_relay(2)
+
+        @job(0, 2)
+        def _():
+            @pl.loop(0, 4)
             def _(i):
-                slopes(ROW_B + i * 256, 256, HALF1, 256)
+                slopes(ROW_O + i * 256, 256, HALF1, 256)
 
             share_column()
-            far_relay(2)
-            next_send(2)
+
+        @job(4, 3)
+        def _():
+            next_send(3)
+            odd_send(3)
+            far_send(3, PIECES)
+
+        @job(1, 4)
+        def _():
+            far_relay(3)
             text_part(second_half, 0, 1024, HALF1, 256, True)
-            odd_send(2)
-            far_relay(3)
 
             @pl.when(k == 1)
             def _():
                 text_part(second_half, ROW_F, N, HALF1, 256, False)
-
             text_part(second_half, ROW_O, 1024, HALF1, 256, False, lambda d, c: g_text(1, d, c).start())
-            far_relay(4)
-
-    next_send(3)
+
+    odd_relay(6)
+    odd_relay(7)
+    far_relay(4)
+    far_relay(5)
 
     @pl.when(k == 0)
     def _():
@@ -480,13 +537,11 @@
     def _(j):
         g_mate(j).start()
 
-    far_relay(5)
-
     image_part(own.at[0], ROW_O, N, N, False)
-    odd_send(3)
+    far_relay(6)
+    share_group()
     text_part(own.at[1], ROW_B + 256, 768, 0, N, False)
-
-    share_group()
+    far_relay(7)
 
     def whole(v):
         return jnp.sum(jnp.sum(v, axis=0, keepdims=True), axis=1, keepdims=True)
@@ -508,7 +563,6 @@
 
     @pl.loop(0, PIECES)
     def _(p):
-        pl.when(p < 2)(lambda: far_relay(p + 6))
         pl.when(p % 2 == 0)(lambda: g_mate(p // 2).wait_recv())
         g_across(p).wait_recv()
 
@@ -563,6 +617,7 @@
     def _(p):
         g_across(p).wait_send()
         pl.when(k == 1)(lambda: g_far5(p).wait_send())
+        pl.when(h1k1 & (p >= TURN))(lambda: g_turn(p).wait_send())
         store(0, p * S, S, p).wait()
 
     for q in range(2):
@@ -622,10 +677,10 @@
             pltpu.VMEM((3, 1, 1), F32),
             dma((6, CHUNKS)),
             dma((5, CHUNKS)),
-            dma((4, PIECES)),
             dma((5, PIECES)),
-            dma((10,)),
-            dma((10,)),
+            dma((5, PIECES)),
+            dma((6,)),
+            dma((6,)),
             dma((8,)),
             dma((8,)),
             dma((16,)),

time: 141 us -> 137 us (0.972)
  Pallas kernels: 139 us -> 135 us
    pallas_call x1, Pallas kernels: 133 us -> 129 us  [shards(): pl.pallas_call(kernel, out_shape=(block, block, one, one, one), in_specs=...]
where the time goes in v4:
time: 137 us
  Pallas kernels  135 us (99%)
  between operations  2.13 us (2%)
    pallas_call x1, Pallas kernels, shards(): pl.pallas_call(kernel, out_shape=(block, block, one, one, one), in_specs=...  129 us
    pallas_call x1, Pallas kernels, shards(): pl.pallas_call(hand_over, out_shape=(block, block, one, one, one), in_spe...  6.04 us

profile of v4, /device:TPU:0, one launch (start us, length us, event | category | flops | bytes accessed | tf_op | source)
XLA Modules:
  0.0 136.9 jit_solution(10200151654233020337)
XLA Ops:
  1.9 128.8 %contrastive_window.1 = (f32[512,1152]{1,0:T(8,128)}, f32[512,1152]{1,0:T(8,128)}, f32[1,1]{1,0:T(1,128)}, f32[1,1]{1,0:T(1,128)}, f32[1,1]{1,0:T(1,128)}) custom-call(f32[1,1]{1,0:T(1,128)} %bitcast.9.scale_ref, f32[1,1]{1,0:T(1,128)} %bitcast.10.offset_ref, f32[512,1152]{1,0:T(8,128)} %bitcast.11, f32[512,1152]{1,0:T(8,128)} %bitcast.12), custom_call_target="tpu_custom_call" | custom-call | tf_op jit(solution)/shard_map/contrastive_window/pallas_call | solution.py:657
  130.7 6.0 %hand_over.1 = (f32[512,1152]{1,0:T(8,128)}, f32[512,1152]{1,0:T(8,128)}, f32[1,1]{1,0:T(1,128)}, f32[1,1]{1,0:T(1,128)}, f32[1,1]{1,0:T(1,128)}) custom-call(f32[512,1152]{1,0:T(8,128)} %get-tuple-element.15.a, f32[512,1152]{1,0:T(8,128)} %get-tuple-element.16.b, f32[1,1]{1,0:T(1,128)} %get-tuple-element.17.c, f32[1,1]{1,0:T(1,128)} %get-tuple-element.18.d, ...), custom_call_target="tpu_custom_call" | custom-call | tf_op jit(solution)/shard_map/hand_over/pallas_call | solution.py:701

commit v5 on v4

--- a/solution.py
+++ b/solution.py
@@ -635,11 +635,12 @@
     def steps(src, here, dst, s):
         return pltpu.make_async_copy(src, here, sem.at[0, s]), pltpu.make_async_copy(here, dst, sem.at[1, s])
 
-    order = [steps(c, held_c, oc, 0), steps(d, held_d, od, 1), steps(e, held_e, oe, 2)]
-    for i in range(CHUNKS):
-        r = pl.ds(i * R, R)
+    order = []
+    for i in range(PIECES):
+        r = pl.ds(i * S, S)
         order.append(steps(a.at[r], held.at[0, r], oa.at[r], 3 + 2 * i))
         order.append(steps(b.at[r], held.at[1, r], ob.at[r], 4 + 2 * i))
+    order += [steps(c, held_c, oc, 0), steps(d, held_d, od, 1), steps(e, held_e, oe, 2)]
     for fetch, _ in order:
         fetch.start()
     for fetch, give in order:
@@ -703,7 +704,7 @@
         out_shape=(block, block, one, one, one),
         in_specs=[any_space] * 5,
         out_specs=(any_space,) * 5,
-        scratch_shapes=[pltpu.VMEM((2, N, D), F32)] + [pltpu.VMEM((1, 1), F32)] * 3 + [dma((2, 3 + 2 * CHUNKS))],
+        scratch_shapes=[pltpu.VMEM((2, N, D), F32)] + [pltpu.VMEM((1, 1), F32)] * 3 + [dma((2, 3 + 2 * PIECES))],
         name="hand_over",
     )(picture, caption, loss, scale_deriv, offset_deriv)
     return (

time: 137 us -> 137 us (level)
  no operation moved by 1% of the time
where the time goes in v5:
time: 137 us
  Pallas kernels  135 us (99%)
  between operations  2.13 us (2%)
    pallas_call x1, Pallas kernels, shards(): pl.pallas_call(kernel, out_shape=(block, block, one, one, one), in_specs=...  129 us
    pallas_call x1, Pallas kernels, shards(): pl.pallas_call(hand_over, out_shape=(block, block, one, one, one), in_spe...  6.3 us

profile of v5, /device:TPU:0, one launch (start us, length us, event | category | flops | bytes accessed | tf_op | source)
XLA Modules:
  0.0 137.2 jit_solution(14616505737802597187)
XLA Ops:
  1.9 128.8 %contrastive_window.1 = (f32[512,1152]{1,0:T(8,128)}, f32[512,1152]{1,0:T(8,128)}, f32[1,1]{1,0:T(1,128)}, f32[1,1]{1,0:T(1,128)}, f32[1,1]{1,0:T(1,128)}) custom-call(f32[1,1]{1,0:T(1,128)} %bitcast.9.scale_ref, f32[1,1]{1,0:T(1,128)} %bitcast.10.offset_ref, f32[512,1152]{1,0:T(8,128)} %bitcast.11, f32[512,1152]{1,0:T(8,128)} %bitcast.12), custom_call_target="tpu_custom_call" | custom-call | tf_op jit(solution)/shard_map/contrastive_window/pallas_call | solution.py:658
  130.7 6.3 %hand_over.1 = (f32[512,1152]{1,0:T(8,128)}, f32[512,1152]{1,0:T(8,128)}, f32[1,1]{1,0:T(1,128)}, f32[1,1]{1,0:T(1,128)}, f32[1,1]{1,0:T(1,128)}) custom-call(f32[512,1152]{1,0:T(8,128)} %get-tuple-element.15.a, f32[512,1152]{1,0:T(8,128)} %get-tuple-element.16.b, f32[1,1]{1,0:T(1,128)} %get-tuple-element.17.c, f32[1,1]{1,0:T(1,128)} %get-tuple-element.18.d, ...), custom_call_target="tpu_custom_call" | custom-call | tf_op jit(solution)/shard_map/hand_over/pallas_call | solution.py:702
